TPU v7x, 32 devices: a whole 2x2x4 slice. The times are simulated.
32 devices in a mesh: groups: 2 (over y), dp: 8 (over z, x), tensor: 2 (over core).
Axes of the slice: x: 2, y: 2, z: 4, core: 2. Of those that a mesh axis runs over, the one named last changes fastest.
Arguments:
- tokens: bfloat16 [16384, 8192], P(('groups', 'dp'), 'tensor'), parts along dimension 0, may hold values from -6 to 6
- key_weight: bfloat16 [8192, 1024], P('tensor'), may hold values from -0.0625 to 0.0625
- down_pool: bfloat16 [80, 64, 8192], P('dp', None, 'tensor'), may hold values from -0.0625 to 0.0625
- up_pool: bfloat16 [80, 64, 1024], P('dp', None, 'tensor'), may hold values from -0.75 to 0.75
- adapter_ids: int32 [16, 4], P('groups'), parts along dimension 0, may hold values from 0 to 79, as said below
- lengths: int32 [16, 4], P(('groups', 'dp')), parts along dimension 0, may hold values from 1 to 512, 1024 in all within a row
- owner_map: int32 [160], P('groups'), parts along dimension 0, may hold values from 0 to 79, as said below
Outputs:
- keys: bfloat16 [16384, 1024], P(('groups', 'dp'), 'tensor'), parts along dimension 0
There are 2 independent parts, one for each index of `groups`. A program takes and returns all parts, laid end to end along the dimension named above; an argument that names none is the same for every part. Nothing has to cross between parts.
Inputs may be any that keep to these rules, and one draw needn't show every extreme that they name: A permutation: adapter a sits in pool slot owner_map[a], held by dp index owner_map[a] // 10. `adapter_ids`: the 4 requests of one row name adapters held by 4 different dp indices.
All inputs are finite; a program needn't handle non-finite values.
Results may differ from a plain program's by a relative error of at most 0.001.
Values may be sent and summed in bfloat16 or wider, within the bound.
No kernel may reach another device: no remote copies, remote signals or barrier semaphores. Data moves between devices by JAX's collectives and lax.ppermute only.
A program may use at most 128 MiB of HBM per device.

v0:
```python
import jax
import jax.numpy as jnp
from jax import lax
from jax.sharding import PartitionSpec as P

ADAPTER_SCALE = 2.0


def shards(tokens, key_weight, down_pool, up_pool, adapter_ids, lengths, owner_map):
    member = lax.axis_index("dp")
    held = down_pool.shape[0]
    rank_width = down_pool.shape[1]
    sizes = lengths[0]
    slots = owner_map[adapter_ids]
    owners = slots // held
    my_slots = lax.dynamic_index_in_dim(slots, member, 0, keepdims=False)
    within = slots % held
    wanted = (owners == member)[:, :, None] & (
        within[:, :, None] == jnp.arange(held, dtype=jnp.int32)[None, None, :]
    )
    picker = jnp.any(wanted, axis=1).astype(jnp.bfloat16)
    send_down = jnp.dot(
        picker, down_pool.reshape(held, -1), preferred_element_type=jnp.float32
    ).astype(jnp.bfloat16)
    send_up = jnp.dot(picker, up_pool.reshape(held, -1), preferred_element_type=jnp.float32).astype(
        jnp.bfloat16
    )
    send_down = send_down.reshape(picker.shape[0], rank_width, -1)
    send_up = send_up.reshape(picker.shape[0], rank_width, -1)
    recv_down, recv_up = (
        lax.all_to_all(send_down, "dp", split_axis=0, concat_axis=0, tiled=True),
        lax.all_to_all(send_up, "dp", split_axis=0, concat_axis=0, tiled=True),
    )
    my_owners = my_slots // held
    req_down = jnp.take(recv_down, my_owners, axis=0)
    req_up = jnp.take(recv_up, my_owners, axis=0)
    partial_code = lax.ragged_dot(
        tokens, jnp.swapaxes(req_down, 1, 2), sizes, preferred_element_type=jnp.float32
    )
    base_part = jnp.dot(tokens, key_weight, preferred_element_type=jnp.float32)
    code = lax.psum(partial_code, "tensor")
    adapter_delta = lax.ragged_dot(
        code,
        req_up.astype(jnp.float32),
        sizes,
        precision=lax.Precision.HIGHEST,
        preferred_element_type=jnp.float32,
    )
    grand_total = lax.psum_scatter(base_part, "tensor", scatter_dimension=1, tiled=True)
    return (grand_total + ADAPTER_SCALE * adapter_delta).astype(jnp.bfloat16)


def solution(mesh):
    placed = (
        P(("groups", "dp"), "tensor"),
        P("tensor", None),
        P("dp", None, "tensor"),
        P("dp", None, "tensor"),
        P("groups", None),
        P(("groups", "dp"), None),
        P("groups"),
    )
    return jax.shard_map(
        shards, mesh=mesh, in_specs=placed, out_specs=P(("groups", "dp"), "tensor"), check_vma=False
    )
```

profile of v0, /device:TPU:0, one launch (start us, length us, event | category | flops | bytes accessed | tf_op | source)
XLA Modules:
  0.0 215.1 jit_solution(3700807818601935730)
XLA Ops:
  6.5 0.8 copy.17
  7.3 0.1 reshape.113
  7.4 0.7 gather_fusion
  8.1 0.1 reshape.112
  8.2 0.1 copy.20
  8.3 0.1 copy.21
  8.4 6.9 %pad.3 = bf16[16,64,4096]{2,1,0:T(8,128)(2,1)} pad(bf16[10,64,4096]{2,1,0:T(8,128)(2,1)} %param.9, bf16[]{:T(256)} %constant.81), padding=0_6x0_0x0_0 | pad | bytes 13631490
  15.3 11.2 %copy.25 = bf16[2,8,64,4096]{3,1,2,0:T(8,128)(2,1)} copy(bf16[2,8,64,4096]{3,2,1,0:T(8,128)(2,1)} %bitcast.40) | data formatting | bytes 16777216
  26.5 0.1 fusion.1
  26.6 4.6 %convolution_convert_fusion = bf16[8,262144]{1,0:T(8,128)(2,1)S(1)} fusion(pred[8,10]{1,0:T(8,128)(4,1)S(1)} %fusion.1, bf16[10,262144]{1,0:T(8,128)(2,1)} %bitcast.39), kind=kOutput, calls=%fused_computation.3 | convolution fusion | flops 44040192 | bytes 9437264 | tf_op jit(solution)/shard_map/dot_general | solution.py:22
  31.2 4.3 %copy.22 = bf16[8,64,4096]{2,1,0:T(8,128)(2,1)} copy(bf16[8,64,4096]{2,0,1:T(8,128)(2,1)S(1)} %bitcast.41) | data formatting | bytes 8388608 | tf_op jit(solution)/shard_map/reshape | solution.py:28
  35.5 7.3 %all-to-all-start = ((bf16[8,64,4096]{2,1,0:T(8,128)(2,1)}), bf16[8,64,4096]{2,1,0:T(8,128)(2,1)}, u32[]{:S(2)}, u32[]{:S(2)}) async-start(bf16[8,64,4096]{2,1,0:T(8,128)(2,1)} %copy.22), calls=%async_computation.1 | async-start | bytes 8388608 | tf_op jit(solution)/shard_map/all_to_all | solution.py:31
  42.7 0.0 all-reduce.2.cloned.1.call-start
  42.8 1.4 ragged-dot-metadata
  44.2 91.8 %all-to-all-done = bf16[8,64,4096]{2,1,0:T(8,128)(2,1)} async-done(((bf16[8,64,4096]{2,1,0:T(8,128)(2,1)}), bf16[8,64,4096]{2,1,0:T(8,128)(2,1)}, u32[]{:S(2)}, u32[]{:S(2)}) %all-to-all-start) | async-done | bytes 4194336 | tf_op jit(solution)/shard_map/all_to_all | solution.py:31
  136.0 2.9 %gather_fusion.1 = bf16[4,64,4096]{2,1,0:T(8,128)(2,1)S(1)} fusion(bf16[8,64,4096]{2,1,0:T(8,128)(2,1)} %all-to-all-done, s32[1024]{0:T(1024)S(1)} %pad_clamp_fusion), kind=kCustom, calls=%fused_computation.1 | custom fusion | bytes 4194320 | tf_op jit(solution)/shard_map/jit(_take)/gather | solution.py:35
  138.9 3.2 %copy.23 = bf16[4,64,4096]{1,2,0:T(8,128)(2,1)} copy(bf16[4,64,4096]{2,1,0:T(8,128)(2,1)S(1)} %gather_fusion.1) | data formatting | bytes 4194304 | tf_op jit(solution)/shard_map/jit(_take)/gather | solution.py:35
  142.0 4.6 %select_bitcast_fusion = bf16[4,4096,64]{2,1,0:T(8,128)(2,1)} fusion(bf16[4,64,4096]{1,2,0:T(8,128)(2,1)} %copy.23, pred[4]{0:T(512)(128)(4,1)S(1)} %get-tuple-element.13), kind=kLoop, calls=%fused_computation.5 | loop fusion | flops 1048576 | bytes 4194308 | tf_op jit(solution)/shard_map/jit(_take)/select_n | solution.py:35
  146.6 12.0 %ragged-dot-none.1 = f32[1024,64]{1,0:T(8,128)} custom-call(s32[1]{0:T(128)} %get-tuple-element.5, s32[5]{0:T(128)} %get-tuple-element.6, s32[7]{0:T(128)} %get-tuple-element.7, s32[7]{0:T(128)} %get-tuple-element.8, s32[1]{0:T(128)} %get-tuple-element.5, bf16[1024,4096]{1,0:T(8,128)(2,1)} %param.7, bf16[4,4096,64]{2,1,0:T(8,128)(2,1)} %select_bitcast_fusion), custom_call_target="tpu_custom_call" | custom-call | flops 536870912 | bytes 10747920 | tf_op jit(solution)/shard_map/ragged_dot_general/ragged-dot-none
  158.6 0.0 all-reduce.2.cloned.1.call-update
  158.7 0.2 reduce-scatter.2.cloned.1.call-start
  158.9 15.2 %fusion.5 = f32[1024,1024]{1,0:T(8,128)} fusion(bf16[1024,4096]{1,0:T(8,128)(2,1)} %param.7, bf16[4096,1024]{1,0:T(8,128)(2,1)} %param.8), kind=kOutput, calls=%fused_computation.29 | convolution fusion | flops 8589934592 | bytes 20971520 | tf_op jit(solution)/shard_map/dot_general | solution.py:40
  174.1 1.1 copy-done.2
  175.2 0.1 pad.4
  175.2 0.6 copy.26
  175.8 0.3 convolution_convert_fusion.1
  176.1 0.2 copy.24
  176.3 17.7 %all_to_all.10 = bf16[8,64,512]{2,1,0:T(8,128)(2,1)S(1)} all-to-all(bf16[8,64,512]{2,1,0:T(8,128)(2,1)S(1)} %copy.24), channel_id=1, replica_groups=mesh['groups'=2,'dp'=8,'tensor'=2] {'dp'}, dimensions={0} | all-to-all | bytes 1048576 | tf_op jit(solution)/shard_map/all_to_all | solution.py:32
  194.0 0.6 gather_fusion.2
  194.5 0.9 select_convert_fusion
  195.5 9.1 %ragged-dot-none = f32[1024,512]{1,0:T(8,128)} custom-call(s32[1]{0:T(128)} %get-tuple-element.5, s32[5]{0:T(128)} %get-tuple-element.6, s32[7]{0:T(128)} %get-tuple-element.7, s32[7]{0:T(128)} %get-tuple-element.8, s32[1]{0:T(128)} %get-tuple-element.5, f32[1024,64]{1,0:T(8,128)} %all-reduce.2.cloned.1.call-done, f32[4,64,512]{2,1,0:T(8,128)} %select_convert_fusion), custom_call_target="tpu_custom_call" | custom-call | flops 67108864 | bytes 2883600 | tf_op jit(solution)/shard_map/ragged_dot_general/ragged-dot-none
  204.6 3.7 %add_convert_fusion = bf16[1024,512]{1,0:T(8,128)(2,1)} fusion(f32[1024,512]{1,0:T(8,128)} %reduce-scatter.2.cloned.1.call-done, f32[1024,512]{1,0:T(8,128)} %ragged-dot-none), kind=kLoop, calls=%fused_computation.6 | loop fusion | flops 1572864 | bytes 5242880 | tf_op jit(solution)/shard_map/convert_element_type | solution.py:50
  (15 shorter events, 0.1 us)
Async XLA Ops:
  6.5 0.9 copy-start
  35.5 100.5 %all-to-all-start = ((bf16[8,64,4096]{2,1,0:T(8,128)(2,1)}), bf16[8,64,4096]{2,1,0:T(8,128)(2,1)}, u32[]{:S(2)}, u32[]{:S(2)}) async-start(bf16[8,64,4096]{2,1,0:T(8,128)(2,1)} %copy.22), calls=%async_computation.1 | async-start | bytes 8388608 | tf_op jit(solution)/shard_map/all_to_all | solution.py:31
  42.7 152.8 %all-reduce.2.cloned.1.call-start = ((), (), s32[]{:S(2)}) async-start(), calls=%async_computation.4 | async-start | bytes 1048576 | tf_op jit(solution)/shard_map/psum | solution.py:41
  158.7 45.9 %reduce-scatter.2.cloned.1.call-start = ((), (), s32[]{:S(2)}) async-start(), calls=%async_computation.3 | async-start | bytes 6291456 | tf_op jit(solution)/shard_map/reduce_scatter | solution.py:49
  174.1 1.1 copy-start.2
  194.5 13.8 %copy-start.1 = (s32[80]{0:T(128)S(1)}, s32[80]{0:T(128)}, u32[]{:S(2)}) copy-start(s32[80]{0:T(128)} %param.13) | copy-start | bytes 964
Sparse Core Ops, SparseCore 0:
  158.8 16.8 all-reduce.1
  178.1 13.2 reduce-scatter.1
where the time goes:
time: 216 us; the launch traced here: 215 us
  waiting for transfers between devices  91.8 us (42%)
  local copies, waits for them, and re-layouts  32.7 us (15%)
  Pallas kernels  22.4 us (10%)
  matrix products  20.1 us (9%)
  blocking collectives  17.7 us (8%)
  between operations  13.5 us (6%)
  other arithmetic  9.42 us (4%)
  starting transfers between devices  7.51 us (3%)
    all_to_all x1, waiting for transfers between devices, shards(): lax.all_to_all(send_down, 'dp', split_axis=0, concat_axis=0, tiled=True)  91.8 us
    another operation x2, Pallas kernels  21.1 us
    unnamed x11, local copies, waits for them, and re-layouts  20.6 us
    all_to_all x1, blocking collectives, shards(): lax.all_to_all(send_up, 'dp', split_axis=0, concat_axis=0, tiled=True)  17.7 us
    dot_general x1, matrix products, shards(): base_part = jnp.dot(tokens, key_weight, preferred_element_type=jnp.float32)  15.2 us
    all_to_all x1, starting transfers between devices, shards(): lax.all_to_all(send_down, 'dp', split_axis=0, concat_axis=0, tiled=True)  7.25 us
    gather x2, local copies, waits for them, and re-layouts, shards(): req_down = jnp.take(recv_down, my_owners, axis=0)  6.03 us
    dot_general x1, matrix products, shards(): jnp.dot(picker, down_pool.reshape(held, -1), preferred_element_type=jnp.f...  4.61 us
  transfers between devices with their start and end apart: 3, of which 1 were waited for; matrix products, arithmetic and copies ran while one was open for 8% of the time, Pallas kernels for 5%

commit v1 on v0

v1 whole, which is shorter than its diff:
```python
import functools

import jax
import jax.numpy as jnp
from jax import lax
from jax.experimental import pallas as pl
from jax.experimental.pallas import tpu as pltpu
from jax.sharding import PartitionSpec as P

ADAPTER_SCALE = 2.0
MIB = 1 << 20


def pick_kernel(index, down, up, out):
    width = down.shape[2]
    out[:, :, :width] = down[...]
    out[:, :, width:] = up[...]


def pick(index, down_pool, up_pool):
    rank, width = down_pool.shape[1:]
    out_width = up_pool.shape[2]
    many = index.shape[0]
    return pl.pallas_call(
        pick_kernel,
        grid_spec=pltpu.PrefetchScalarGridSpec(
            num_scalar_prefetch=1,
            grid=(many,),
            in_specs=[
                pl.BlockSpec((1, rank, width), lambda j, index: (index[j], 0, 0)),
                pl.BlockSpec((1, rank, out_width), lambda j, index: (index[j], 0, 0)),
            ],
            out_specs=pl.BlockSpec((1, rank, width + out_width), lambda j, index: (j, 0, 0)),
        ),
        out_shape=jax.ShapeDtypeStruct((many, rank, width + out_width), down_pool.dtype),
        name="pick",
    )(index, down_pool, up_pool)


def request_of_rows(ends, count, first, rows):
    at = first + lax.broadcasted_iota(jnp.int32, (rows, 1), 0)
    which = jnp.zeros((rows, 1), jnp.int32)
    for r in range(count - 1):
        which += (at >= ends[r]).astype(jnp.int32)
    return which


def code_kernel(count, place, ends, tokens, *refs):
    blocks, out, down = refs[:count], refs[count], refs[count + 1]
    rank = out.shape[1]

    @pl.when(pl.program_id(0) == 0)
    def _():
        for r in range(count):
            down[r * rank : (r + 1) * rank, :] = blocks[r][0]

    rows = tokens.shape[0]
    full = lax.dot_general(
        tokens[...], down[...], (((1,), (1,)), ((), ())), preferred_element_type=jnp.float32
    )
    which = request_of_rows(ends, count, pl.program_id(0) * rows, rows)
    code = jnp.zeros((rows, rank), jnp.float32)
    for r in range(count):
        code = jnp.where(which == r, full[:, r * rank : (r + 1) * rank], code)
    out[...] = code


def codes(place, ends, tokens, blocks, width):
    many, features = tokens.shape
    count = place.shape[0]
    rank = blocks.shape[1]
    tile = min(256, many)
    return pl.pallas_call(
        functools.partial(code_kernel, count),
        grid_spec=pltpu.PrefetchScalarGridSpec(
            num_scalar_prefetch=2,
            grid=(many // tile,),
            in_specs=[pl.BlockSpec((tile, features), lambda i, place, ends: (i, 0))]
            + [
                pl.BlockSpec((1, rank, width), lambda i, place, ends, r=r: (place[r], 0, 0))
                for r in range(count)
            ],
            out_specs=pl.BlockSpec((tile, rank), lambda i, place, ends: (i, 0)),
            scratch_shapes=[pltpu.VMEM((count * rank, width), blocks.dtype)],
        ),
        out_shape=jax.ShapeDtypeStruct((many, rank), jnp.float32),
        compiler_params=pltpu.CompilerParams(vmem_limit_bytes=40 * MIB),
        name="codes",
    )(place, ends, tokens, *([blocks] * count))


def finish_kernel(count, parts, place, ends, *refs):
    code_parts, base_parts = refs[:parts], refs[parts : 2 * parts]
    blocks = refs[2 * parts : 2 * parts + count]
    out = refs[2 * parts + count]
    up = refs[2 * parts + count + 1]
    rank = blocks[0].shape[1]

    @pl.when(pl.program_id(0) == 0)
    def _():
        for r in range(count):
            up[r * rank : (r + 1) * rank, :] = blocks[r][0]

    rows = out.shape[0]
    code = code_parts[0][...]
    base = base_parts[0][...]
    for p in range(1, parts):
        code = code + code_parts[p][...]
        base = base + base_parts[p][...]
    which = request_of_rows(ends, count, pl.program_id(0) * rows, rows)
    zero = jnp.zeros_like(code)
    wide = jnp.concatenate([jnp.where(which == r, code, zero) for r in range(count)], axis=1)
    delta = None
    for _ in range(3):
        part = wide.astype(jnp.bfloat16)
        wide = wide - part.astype(jnp.float32)
        term = jnp.dot(part, up[...], preferred_element_type=jnp.float32)
        delta = term if delta is None else delta + term
    out[...] = (base + ADAPTER_SCALE * delta).astype(out.dtype)


def finish(place, ends, code_parts, base_parts, blocks, width):
    many, rank = code_parts[0].shape
    columns = base_parts[0].shape[1]
    count = place.shape[0]
    parts = len(code_parts)
    tile = min(256, many)
    return pl.pallas_call(
        functools.partial(finish_kernel, count, parts),
        grid_spec=pltpu.PrefetchScalarGridSpec(
            num_scalar_prefetch=2,
            grid=(many // tile,),
            in_specs=[pl.BlockSpec((tile, rank), lambda i, place, ends: (i, 0))] * parts
            + [pl.BlockSpec((tile, columns), lambda i, place, ends: (i, 0))] * parts
            + [
                pl.BlockSpec(
                    (1, rank, columns),
                    lambda i, place, ends, r=r: (place[r], 0, width // columns),
                )
                for r in range(count)
            ],
            out_specs=pl.BlockSpec((tile, columns), lambda i, place, ends: (i, 0)),
            scratch_shapes=[pltpu.VMEM((count * rank, columns), blocks.dtype)],
        ),
        out_shape=jax.ShapeDtypeStruct((many, columns), jnp.bfloat16),
        compiler_params=pltpu.CompilerParams(vmem_limit_bytes=32 * MIB),
        name="finish",
    )(place, ends, *code_parts, *base_parts, *([blocks] * count))


def gathered(parts, axis, sizes):
    held = [parts]
    for step in range(1, sizes):
        held.append(lax.ppermute(parts, axis, [(i, (i + step) % sizes) for i in range(sizes)]))
    return held


def shards(n_tensor, tokens, key_weight, down_pool, up_pool, adapter_ids, lengths, owner_map):
    member = lax.axis_index("dp")
    held, _, width = down_pool.shape
    columns = up_pool.shape[2]
    slots = owner_map[adapter_ids]
    owners = slots // held
    within = slots % held
    send_index = jnp.sum(jnp.where(owners == member, within, 0), axis=1).astype(jnp.int32)
    my_owners = lax.dynamic_index_in_dim(owners, member, 0, keepdims=False)
    ends = jnp.cumsum(lengths[0]).astype(jnp.int32)

    send = pick(send_index, down_pool, up_pool)
    blocks = lax.all_to_all(send, "dp", split_axis=0, concat_axis=0, tiled=True)

    me = lax.axis_index("tensor")
    base_parts = []
    for step in range(n_tensor):
        to = lax.rem(me + step, n_tensor)
        weight = lax.dynamic_slice_in_dim(key_weight, to * columns, columns, 1)
        part = jnp.dot(tokens, weight, preferred_element_type=jnp.float32)
        if step:
            part = lax.ppermute(
                part, "tensor", [(i, (i + step) % n_tensor) for i in range(n_tensor)]
            )
        base_parts.append(part)

    code = codes(my_owners, ends, tokens, blocks, width)
    code_parts = gathered(code, "tensor", n_tensor)
    return finish(my_owners, ends, code_parts, base_parts, blocks, width)


def solution(mesh):
    placed = (
        P(("groups", "dp"), "tensor"),
        P("tensor", None),
        P("dp", None, "tensor"),
        P("dp", None, "tensor"),
        P("groups", None),
        P(("groups", "dp"), None),
        P("groups"),
    )
    return jax.shard_map(
        functools.partial(shards, mesh.shape["tensor"]),
        mesh=mesh,
        in_specs=placed,
        out_specs=P(("groups", "dp"), "tensor"),
        check_vma=False,
    )
```

time: 216 us -> 142 us (0.66)
  the two profiles are of different devices: /device:TPU:0 before, /device:TPU:1 now
where the time goes in v1:
time: 142 us
  waiting for transfers between devices  92.1 us (65%)
  Pallas kernels  18.2 us (13%)
  matrix products  16.9 us (12%)
  starting transfers between devices  8.66 us (6%)
  local copies, waits for them, and re-layouts  5.18 us (4%)
    all_to_all x1, waiting for transfers between devices, shards(): blocks = lax.all_to_all(send, 'dp', split_axis=0, concat_axis=0, tiled=True)  92.1 us
    dot_general x2, matrix products, shards(): part = jnp.dot(tokens, weight, preferred_element_type=jnp.float32)  16.9 us
    pallas_call x1, Pallas kernels, pick(): pl.pallas_call(pick_kernel, grid_spec=pltpu.PrefetchScalarGridSpec(num_sc...  7.48 us
    pallas_call x1, Pallas kernels, codes(): pl.pallas_call(functools.partial(code_kernel, count), grid_spec=pltpu.Pre...  6.37 us
    all_to_all x1, starting transfers between devices, shards(): blocks = lax.all_to_all(send, 'dp', split_axis=0, concat_axis=0, tiled=True)  5.82 us
    pallas_call x1, Pallas kernels, finish(): pl.pallas_call(functools.partial(finish_kernel, count, parts), grid_spec=...  4.34 us
    unnamed x7, local copies, waits for them, and re-layouts  4.16 us
  transfers between devices with their start and end apart: 3, of which 1 were waited for; matrix products, arithmetic and copies ran while one was open for 12% of the time, Pallas kernels for 4%

profile of v1, /device:TPU:1, one launch (start us, length us, event | category | flops | bytes accessed | tf_op | source)
XLA Modules:
  0.0 142.0 jit_solution(4024258826440792406)
XLA Ops:
  0.0 0.0 copy-start
  0.0 0.8 copy.13
  0.8 0.1 reshape.31
  0.9 0.0 copy-done
  0.9 0.7 gather_fusion
  1.6 0.1 reshape.41
  1.7 0.1 reshape.43
  1.8 0.1 reshape.45
  1.8 0.6 fusion.11
  2.5 7.5 %pick.1 = bf16[8,64,4608]{2,1,0:T(8,128)(2,1)} custom-call(s32[8]{0:T(128)} %get-tuple-element.5.index, bf16[10,64,4096]{2,1,0:T(8,128)(2,1)} %down.1, bf16[10,64,512]{2,1,0:T(8,128)(2,1)} %up.1), custom_call_target="tpu_custom_call" | custom-call | tf_op jit(solution)/shard_map/pick/pallas_call | solution.py:24
  10.0 5.8 %all-to-all-start = ((bf16[8,64,4608]{2,1,0:T(8,128)(2,1)}), bf16[8,64,4608]{2,1,0:T(8,128)(2,1)}, u32[]{:S(2)}, u32[]{:S(2)}) async-start(bf16[8,64,4608]{2,1,0:T(8,128)(2,1)} %pick.1), calls=%async_computation | async-start | bytes 9437184 | tf_op jit(solution)/shard_map/all_to_all | solution.py:170
  15.8 0.0 copy-start.2
  15.8 10.4 %fusion.7 = f32[1024,512]{1,0:T(8,128)} fusion(bf16[1024,4096]{1,0:T(8,128)(2,1)} %tokens.1, bf16[4096,1024]{1,0:T(8,128)(2,1)} %param.8, s32[]{:T(128)S(6)} %select_n.35), kind=kOutput, calls=%fused_computation.6 | convolution fusion | flops 4294967296 | bytes 14680068 | tf_op jit(solution)/shard_map/dot_general | solution.py:177
  26.2 1.0 collective-permute-start.1
  27.1 0.0 copy-done.2
  27.1 0.2 reduce-window.9
  27.3 92.1 %all-to-all-done.refs_0_.refs_1_.refs_2_.refs_3_.refs_4_.refs_5_.refs_6_.refs_7_ = bf16[8,64,4608]{2,1,0:T(8,128)(2,1)} async-done(((bf16[8,64,4608]{2,1,0:T(8,128)(2,1)}), bf16[8,64,4608]{2,1,0:T(8,128)(2,1)}, u32[]{:S(2)}, u32[]{:S(2)}) %all-to-all-start) | async-done | bytes 4718624 | tf_op jit(solution)/shard_map/all_to_all | solution.py:170
  119.5 0.0 copy-start.1
  119.5 3.4 %copy-done.1 = bf16[1024,4096]{1,0:T(8,128)(2,1)S(1)} copy-done((bf16[1024,4096]{1,0:T(8,128)(2,1)S(1)}, bf16[1024,4096]{1,0:T(8,128)(2,1)}, u32[]{:S(2)}) %copy-start.1) | copy-done | bytes 8388632
  122.8 6.4 %codes.1.refs_0_ = f32[1024,64]{1,0:T(8,128)S(1)} custom-call(s32[4]{0:T(128)S(1)} %fusion.14.place, s32[4]{0:T(128)S(1)} %bitcast.10, bf16[1024,4096]{1,0:T(8,128)(2,1)S(1)} %copy-done.1, bf16[8,64,4608]{2,1,0:T(8,128)(2,1)} %all-to-all-done.refs_0_.refs_1_.refs_2_.refs_3_.refs_4_.refs_5_.refs_6_.refs_7_, ...), custom_call_target="tpu_custom_call" | custom-call | tf_op jit(solution)/shard_map/codes/pallas_call | solution.py:73
  129.2 1.9 %collective-permute-start = (f32[1024,64]{1,0:T(8,128)S(1)}, f32[1024,64]{1,0:T(8,128)S(1)}, u32[]{:S(2)}, u32[]{:S(2)}) collective-permute-start(f32[1024,64]{1,0:T(8,128)S(1)} %codes.1.refs_0_), channel_id=1, source_target_pairs={{0,1},{1,0},{2,3},{3,2},{4,5},{5,4},{6,7},{7,6},{8,9},{9,8},{10,11... | collective-permute-start | bytes 786440 | tf_op jit(solution)/shard_map/ppermute | solution.py:154
  131.1 6.6 %fusion.4.refs_2_ = f32[1024,512]{1,0:T(8,128)S(1)} fusion(bf16[1024,4096]{1,0:T(8,128)(2,1)S(1)} %copy-done.1, bf16[4096,1024]{1,0:T(8,128)(2,1)} %param.8, s32[]{:T(128)S(6)} %select_n.34), kind=kOutput, calls=%fused_computation.5 | convolution fusion | flops 4294967296 | bytes 14680068 | tf_op jit(solution)/shard_map/dot_general | solution.py:177
  137.7 0.0 collective-permute-done.1.refs_3_
  137.7 0.0 collective-permute-done.refs_1_
  137.7 4.3 %finish.1 = bf16[1024,512]{1,0:T(8,128)(2,1)} custom-call(s32[4]{0:T(128)S(1)} %fusion.14.place, s32[4]{0:T(128)S(1)} %bitcast.11, f32[1024,64]{1,0:T(8,128)S(1)} %codes.1.refs_0_, f32[1024,64]{1,0:T(8,128)S(1)} %collective-permute-done.refs_1_, f32[1024,512]{1,0:T(8,128)S(1)} %fusion.4.refs_2_, f32[1024,512]{1,0:T(8,128)S(1)} %collective-permute-done.1.refs_3_, ...), custom_call_target="tpu_custom_call" | custom-call | tf_op jit(solution)/shard_map/finish/pallas_call | solution.py:128
  (5 shorter events, 0.0 us)
Async XLA Ops:
  0.0 0.9 copy-start
  10.0 109.5 %all-to-all-start = ((bf16[8,64,4608]{2,1,0:T(8,128)(2,1)}), bf16[8,64,4608]{2,1,0:T(8,128)(2,1)}, u32[]{:S(2)}, u32[]{:S(2)}) async-start(bf16[8,64,4608]{2,1,0:T(8,128)(2,1)} %pick.1), calls=%async_computation | async-start | bytes 9437184 | tf_op jit(solution)/shard_map/all_to_all | solution.py:170
  15.8 11.3 %copy-start.2 = (s32[1,4]{1,0:T(1,128)S(1)}, s32[1,4]{1,0:T(1,128)}, u32[]{:S(2)}) copy-start(s32[1,4]{1,0:T(1,128)} %param.12) | copy-start | bytes 52
  26.2 111.5 %collective-permute-start.1 = (f32[1024,512]{1,0:T(8,128)}, f32[1024,512]{1,0:T(8,128)S(1)}, u32[]{:S(2)}, u32[]{:S(2)}) collective-permute-start(f32[1024,512]{1,0:T(8,128)} %fusion.7), channel_id=1, source_target_pairs={{0,1},{1,0},{2,3},{3,2},{4,5},{5,4},{6,7},{7,6},{8,9},{9,8},{10,11... | collective-permute-start | bytes 6291464 | tf_op jit(solution)/shard_map/ppermute | solution.py:179
  119.5 3.4 %copy-start.1 = (bf16[1024,4096]{1,0:T(8,128)(2,1)S(1)}, bf16[1024,4096]{1,0:T(8,128)(2,1)}, u32[]{:S(2)}) copy-start(bf16[1024,4096]{1,0:T(8,128)(2,1)} %tokens.1) | copy-start | bytes 25165828
  129.2 8.5 %collective-permute-start = (f32[1024,64]{1,0:T(8,128)S(1)}, f32[1024,64]{1,0:T(8,128)S(1)}, u32[]{:S(2)}, u32[]{:S(2)}) collective-permute-start(f32[1024,64]{1,0:T(8,128)S(1)} %codes.1.refs_0_), channel_id=1, source_target_pairs={{0,1},{1,0},{2,3},{3,2},{4,5},{5,4},{6,7},{7,6},{8,9},{9,8},{10,11... | collective-permute-start | bytes 786440 | tf_op jit(solution)/shard_map/ppermute | solution.py:154

commit v2 on v1

--- a/solution.py
+++ b/solution.py
@@ -155,19 +155,300 @@
     return held
 
 
-def shards(n_tensor, tokens, key_weight, down_pool, up_pool, adapter_ids, lengths, owner_map):
+Z_STEPS = 10
+X_STEPS = 11
+
+
+def route(slots, held, planes):
+    rows, req = slots.shape
+    n = rows * req
+    item = jnp.arange(n, dtype=jnp.int32)
+    slot = slots.reshape(n)
+    row = item // req
+    dest, side = row // 2, row % 2
+    owner = slot // held
+    src, col = owner // 2, owner % 2
+    same = slot[:, None] == slot[None, :]
+    far = dest != src
+    xkey = jnp.where(far, jnp.abs(dest - src) * n + (n - 1 - item), -1)
+    slot_key = jnp.max(jnp.where(same, xkey[None, :], -1), axis=1)
+    xlead = far & (xkey == slot_key)
+    ahead = xlead[None, :] & (owner[None, :] == owner[:, None]) & (xkey[None, :] > slot_key[:, None])
+    xpos = jnp.sum(ahead.astype(jnp.int32), axis=1)
+    d_dest = jnp.stack([dest, planes - 1 - dest])
+    d_src = jnp.stack([src, planes - 1 - src])
+    going = d_dest > d_src
+    zkey = jnp.where(going, d_dest * n + (n - 1 - item)[None, :], -1)
+    lead = going & (zkey == jnp.max(jnp.where(same[None], zkey[:, None, :], -1), axis=2))
+    columns = jnp.arange(2, dtype=jnp.int32)[:, None]
+    first = jnp.where(col[None, :] == columns, 0, xpos[None, :] + 1)[:, None, :]
+    links, arrivals = [], []
+    for p in range(planes - 1):
+        on = (lead & (d_src <= p) & (d_dest > p))[None]
+        starts = (d_src == p)[None]
+        ready = first if p == 0 else jnp.where(starts, first, links[-1][1] + 1)
+        key = (ready * planes + (planes - d_dest)[None]) * n + item
+        before = on[:, :, None, :] & (key[:, :, None, :] <= key[:, :, :, None])
+        rank = jnp.sum(before.astype(jnp.int32), axis=3)
+        pos = jnp.max(
+            jnp.where(before, ready[:, :, None, :] - rank[:, :, None, :], -n), axis=3
+        ) + rank
+        links.append((jnp.broadcast_to(on, pos.shape), pos))
+        arrivals.append(
+            jnp.max(jnp.where(on[:, :, None, :] & same, pos[:, :, None, :], -1), axis=3)
+        )
+    arrival = arrivals[0]
+    for p in range(1, planes - 1):
+        arrival = jnp.where((d_dest == p + 1)[None], arrivals[p], arrival)
+    arrival = jnp.where(going[0], arrival[:, 0], arrival[:, 1])
+    shape = (rows, req)
+    partner_col = 1 - jnp.arange(rows, dtype=jnp.int32)[:, None] % 2
+    partner = jnp.arange(rows, dtype=jnp.int32)[:, None] // 2 * 2 + partner_col
+    sent = jnp.max(
+        jnp.where(xlead[None, :] & (owner[None, :] == partner), xpos[None, :] + 1, 0), axis=1
+    )[:, None]
+    by_partner = jnp.where(side == 0, arrival[1], arrival[0]).reshape(shape)
+    near = ~far.reshape(shape)
+    from_partner = near & (col.reshape(shape) == partner_col)
+    ready = jnp.where(near, sent, jnp.maximum(sent, by_partner + 1))
+    ready = jnp.stack([ready, ready], axis=2).reshape(rows, 2 * req)
+    valid = jnp.stack([from_partner | ~near, from_partner], axis=2).reshape(rows, 2 * req)
+    key = ready * (2 * req) + jnp.arange(2 * req, dtype=jnp.int32)[None, :]
+    before = valid[:, None, :] & (key[:, None, :] <= key[:, :, None])
+    rank = jnp.sum(before.astype(jnp.int32), axis=2)
+    dpos = jnp.max(jnp.where(before, ready[:, None, :] - rank[:, None, :], -n), axis=2) + rank
+    need_x = jnp.max(jnp.maximum(jnp.where(valid, dpos + 1, 0), sent))
+    need_z = functools.reduce(
+        jnp.maximum, [jnp.max(jnp.where(on, pos + 1, 0)) for on, pos in links]
+    )
+    return dict(
+        row=row, dest=dest, owner=owner, src=src, col=col, far=far, within=slot % held,
+        going=going, lead=lead, d_src=d_src, xpos=xpos, links=links, arrival=arrival,
+        dpos=dpos, valid=valid, need_x=need_x, need_z=need_z,
+    )
+
+
+def tables(slots, held, planes, member):
+    rows, req = slots.shape
+    plan = route(slots, held, planes)
+    plane, column = member // 2, member % 2
+    over_x, from_z = 2 * held, 2 * held + X_STEPS
+    pool = 2 * plan["within"]
+    arrived = jnp.where(column == 0, plan["arrival"][0], plan["arrival"][1])
+    via_z = from_z + jnp.where(plan["going"][0], 0, Z_STEPS) + arrived
+
+    def table(steps, *entries):
+        step = jnp.arange(steps, dtype=jnp.int32)[:, None]
+        best = jnp.full((steps,), -1, jnp.int32)
+        for on, pos, source in entries:
+            hit = on[None, :] & (pos[None, :] == step)
+            best = jnp.maximum(best, jnp.max(jnp.where(hit, source[None, :], -1), axis=1))
+        return best
+
+    mine = plan["far"] & (plan["owner"] == member)
+    other = member + 1 - 2 * column
+    to_other = plan["row"] == other
+    dpos = plan["dpos"].reshape(-1, 2)
+    valid = plan["valid"].reshape(-1, 2)
+    x_send = table(
+        X_STEPS,
+        (mine, plan["xpos"], pool + 1 - column),
+        (to_other & valid[:, 0], dpos[:, 0], jnp.where(plan["far"], via_z, pool)),
+        (to_other & valid[:, 1], dpos[:, 1], pool + 1),
+    )
+    z_send = []
+    for d in range(2):
+        at = plane if d == 0 else planes - 1 - plane
+        source = jnp.where(plan["col"] == column, pool + column, over_x + plan["xpos"])
+        on = jnp.zeros_like(plan["far"])
+        pos = jnp.zeros_like(plan["xpos"])
+        for p in range(planes - 1):
+            link_on = plan["links"][p][0][:, d]
+            link_pos = plan["links"][p][1][:, d]
+            here = at == p
+            on = jnp.where(here, jnp.where(column == 0, link_on[0], link_on[1]), on)
+            pos = jnp.where(here, jnp.where(column == 0, link_pos[0], link_pos[1]), pos)
+            if p:
+                last = plan["links"][p - 1][1][:, d]
+                last = jnp.where(column == 0, last[0], last[1])
+                passing = here & (plan["d_src"][d] < p)
+                source = jnp.where(passing, from_z + d * Z_STEPS + last, source)
+        z_send.append(table(Z_STEPS, (on, pos, source)))
+    halves = []
+    for h in range(2):
+        near = jnp.where(plan["col"] == column, pool + h, over_x + dpos[:, h])
+        far = jnp.where(column == h, via_z, over_x + dpos[:, 0])
+        halves.append(jnp.where(plan["far"], far, near))
+    place = jnp.stack(halves, axis=1).reshape(rows, 2 * req)
+    place = lax.dynamic_index_in_dim(place, member, 0, keepdims=False)
+    fits = (plan["need_x"] <= X_STEPS) & (plan["need_z"] <= Z_STEPS)
+    x_send, up_send, down_send = [jnp.where(fits, t, -1) for t in (x_send, *z_send)]
+    return x_send, up_send, down_send, place, fits
+
+
+def copies(code, base_code, down, up, arrays, out, rows, sem):
+    width = down.shape[2]
+    lo, size = rows
+    held = down.shape[0]
+    slot, half = code // 2, code % 2
+    start = pl.multiple_of(half * (down.shape[1] // 2) + lo, size)
+    slot = jnp.clip(slot, 0, held - 1)
+    pool = [
+        pltpu.make_async_copy(
+            down.at[slot, pl.ds(start, size), :], out.at[:, pl.ds(0, width)], sem
+        ),
+        pltpu.make_async_copy(
+            up.at[slot, pl.ds(start, size), :], out.at[:, pl.ds(width, up.shape[2])], sem
+        ),
+    ]
+    pairs = [((code >= 0) & (code < 2 * held), pool)]
+    for number, array in arrays:
+        pairs.append((code == number, [pltpu.make_async_copy(array, out, sem)]))
+    return pairs
+
+
+def send_kernel(step, sub, size, codes, down, up, *refs):
+    n = 3 * step
+    x_in, up_in, down_in = refs[:step], refs[step : 2 * step], refs[2 * step : n]
+    outs = refs[n:-1]
+    sem = refs[-1]
+    base = 2 * down.shape[0]
+    from_x = [(base + s, r) for s, r in enumerate(x_in)]
+    from_below = [(base + X_STEPS + s, r) for s, r in enumerate(up_in)]
+    from_above = [(base + X_STEPS + Z_STEPS + s, r) for s, r in enumerate(down_in)]
+    sources = [from_below + from_above, from_x + from_below, from_x + from_above]
+    rows = (sub * size, size)
+    for i, out in enumerate(outs):
+        for on, list_of in copies(codes[i], base, down, up, sources[i], out, rows, sem.at[i]):
+
+            @pl.when(on)
+            def _(list_of=list_of):
+                for c in list_of:
+                    c.start()
+
+    for i, out in enumerate(outs):
+
+        @pl.when(codes[i] >= 0)
+        def _(i=i, out=out):
+            pltpu.make_async_copy(out, out, sem.at[i]).wait()
+
+
+ANY = pl.BlockSpec(memory_space=pl.ANY)
+
+
+def pick_step(step, sub, size, codes, down, up, got):
+    width = down.shape[2] + up.shape[2]
+    outs = 3 if step < Z_STEPS else 1
+    return pl.pallas_call(
+        functools.partial(send_kernel, step, sub, size),
+        grid_spec=pltpu.PrefetchScalarGridSpec(
+            num_scalar_prefetch=1,
+            grid=(),
+            in_specs=[ANY] * (2 + 3 * step),
+            out_specs=[ANY] * outs,
+            scratch_shapes=[pltpu.SemaphoreType.DMA((3,))],
+        ),
+        out_shape=[jax.ShapeDtypeStruct((size, width), down.dtype)] * outs,
+        name="pick_step",
+    )(codes, down, up, *got[0], *got[1], *got[2])
+
+
+def collect_kernel(req, size, n_x, n_z, codes, down, up, *refs):
+    n = n_x + 2 * n_z
+    a_in, b_in, out, sem = refs[:n], refs[n : 2 * n], refs[2 * n], refs[2 * n + 1]
+    base = 2 * down.shape[0]
+    half_rows = down.shape[1] // 2
+    for r in range(req):
+        for h in range(2):
+            code = codes[2 * r + h]
+            todo = []
+            for sub, arrays in enumerate((a_in, b_in)):
+                target = out.at[r, pl.ds(h * half_rows + sub * size, size), :]
+                sources = [(base + k, a) for k, a in enumerate(arrays)]
+                todo.append(
+                    copies(code, base, down, up, sources, target, (sub * size, size), sem.at[r])
+                )
+            for (on, first), (_, second) in zip(*todo):
+
+                @pl.when(on)
+                def _(first=first, second=second):
+                    for c in first + second:
+                        c.start()
+
+    for r in range(req):
+        pltpu.make_async_copy(out.at[r], out.at[r], sem.at[r]).wait()
+
+
+def collect(size, codes, down, up, got_a, got_b):
+    req = codes.shape[0] // 2
+    rank = down.shape[1]
+    width = down.shape[2] + up.shape[2]
+    flat = [a for got in (got_a, got_b) for stream in got for a in stream]
+    return pl.pallas_call(
+        functools.partial(collect_kernel, req, size, len(got_a[0]), len(got_a[1])),
+        grid_spec=pltpu.PrefetchScalarGridSpec(
+            num_scalar_prefetch=1,
+            grid=(),
+            in_specs=[ANY] * (2 + len(flat)),
+            out_specs=ANY,
+            scratch_shapes=[pltpu.SemaphoreType.DMA((req,))],
+        ),
+        out_shape=jax.ShapeDtypeStruct((req, rank, width), down.dtype),
+        name="collect",
+    )(codes, down, up, *flat)
+
+
+def dense(slots, held, member, down_pool, up_pool):
+    owners = slots // held
+    index = jnp.sum(jnp.where(owners == member, slots % held, 0), axis=1).astype(jnp.int32)
+    my_owners = lax.dynamic_index_in_dim(owners, member, 0, keepdims=False)
+    send = pick(index, down_pool, up_pool)
+    blocks = lax.all_to_all(send, "dp", split_axis=0, concat_axis=0, tiled=True)
+    return jnp.take(blocks, my_owners, axis=0, mode="clip")
+
+
+def routed(n_groups, slots, held, planes, member, down_pool, up_pool, work):
+    rank = down_pool.shape[1]
+    size = rank // 4
+    x_send, up_send, down_send, place, fits = tables(slots, held, planes, member)
+    misfit = 1 - fits.astype(jnp.int32).reshape(1)
+    for other in gathered(misfit, "groups", n_groups)[1:]:
+        misfit = jnp.maximum(misfit, other)
+    n = 2 * planes
+    pairs = (
+        [(i, i ^ 1) for i in range(n)],
+        [(i, i + 2) for i in range(n - 2)],
+        [(i + 2, i) for i in range(n - 2)],
+    )
+    got = [([], [], []), ([], [], [])]
+    for step in range(X_STEPS):
+        codes = [x_send[step]]
+        if step < Z_STEPS:
+            codes += [up_send[step], down_send[step]]
+        codes = jnp.stack(codes)
+        for sub in range(2):
+            known = [s[:step] for s in got[sub]]
+            sends = pick_step(step, sub, size, codes, down_pool, up_pool, known)
+            for stream, send, pair in zip(got[sub], sends, pairs):
+                stream.append(lax.ppermute(send, "dp", pair))
+    flat = [a for g in got for s in g for a in s]
+
+    def fast():
+        return collect(size, place, down_pool, up_pool, got[0], got[1])
+
+    def slow():
+        return dense(slots, held, member, down_pool, up_pool)
+
+    return lax.cond(misfit[0] == 0, fast, slow)
+
+
+def shards(sizes, tokens, key_weight, down_pool, up_pool, adapter_ids, lengths, owner_map):
+    n_groups, n_dp, n_tensor = sizes
     member = lax.axis_index("dp")
-    held, _, width = down_pool.shape
+    held, rank, width = down_pool.shape
     columns = up_pool.shape[2]
     slots = owner_map[adapter_ids]
-    owners = slots // held
-    within = slots % held
-    send_index = jnp.sum(jnp.where(owners == member, within, 0), axis=1).astype(jnp.int32)
-    my_owners = lax.dynamic_index_in_dim(owners, member, 0, keepdims=False)
     ends = jnp.cumsum(lengths[0]).astype(jnp.int32)
-
-    send = pick(send_index, down_pool, up_pool)
-    blocks = lax.all_to_all(send, "dp", split_axis=0, concat_axis=0, tiled=True)
 
     me = lax.axis_index("tensor")
     base_parts = []
@@ -181,9 +462,14 @@
             )
         base_parts.append(part)
 
-    code = codes(my_owners, ends, tokens, blocks, width)
+    if n_dp == 8 and rank % 64 == 0:
+        blocks = routed(n_groups, slots, held, n_dp // 2, member, down_pool, up_pool, None)
+    else:
+        blocks = dense(slots, held, member, down_pool, up_pool)
+    place = jnp.arange(slots.shape[1], dtype=jnp.int32)
+    code = codes(place, ends, tokens, blocks, width)
     code_parts = gathered(code, "tensor", n_tensor)
-    return finish(my_owners, ends, code_parts, base_parts, blocks, width)
+    return finish(place, ends, code_parts, base_parts, blocks, width)
 
 
 def solution(mesh):
@@ -196,8 +482,9 @@
         P(("groups", "dp"), None),
         P("groups"),
     )
+    sizes = tuple(mesh.shape[name] for name in ("groups", "dp", "tensor"))
     return jax.shard_map(
-        functools.partial(shards, mesh.shape["tensor"]),
+        functools.partial(shards, sizes),
         mesh=mesh,
         in_specs=placed,
         out_specs=P(("groups", "dp"), "tensor"),

time: 142 us -> 483 us (3.40)
  the two profiles are of different devices: /device:TPU:1 before, /device:TPU:9 now
where the time goes in v2:
time: 483 us; the launch traced here: 476 us
  Pallas kernels  251 us (52%)
  starting transfers between devices  159 us (33%)
  other arithmetic  31.6 us (7%)
  matrix products  16.9 us (3%)
  local copies, waits for them, and re-layouts  9.68 us (2%)
    pallas_call x22, Pallas kernels, pick_step(): pl.pallas_call(functools.partial(send_kernel, step, sub, size), grid_spec...  170 us
    ppermute x62, starting transfers between devices, routed(): stream.append(lax.ppermute(send, 'dp', pair))  140 us
    pallas_call x1, Pallas kernels, collect(): pl.pallas_call(functools.partial(collect_kernel, req, size, len(got_a[0])...  71.3 us
    another operation x10, other arithmetic, routed(): codes = jnp.stack(codes)  24.6 us
    dot_general x2, matrix products, shards(): part = jnp.dot(tokens, weight, preferred_element_type=jnp.float32)  16.9 us
    ppermute x1, starting transfers between devices, shards(): lax.ppermute(part, 'tensor', [(i, (i + step) % n_tensor) for i in range(n...  13.5 us
  transfers between devices with their start and end apart: 65, of which 2 were waited for; matrix products, arithmetic and copies ran while one was open for 8% of the time, Pallas kernels for 49%

profile of v2, /device:TPU:9, one launch (start us, length us, event | category | flops | bytes accessed | tf_op | source)
XLA Modules:
  0.0 476.4 jit_solution(3707508419278424431)
XLA Ops:
  17.3 13.7 %pick_step.33 = (bf16[16,4608]{1,0:T(8,128)(2,1)}, bf16[16,4608]{1,0:T(8,128)(2,1)}, bf16[16,4608]{1,0:T(8,128)(2,1)}) custom-call(s32[3]{0:T(128)} %pad_add_fusion.7.codes, bf16[10,64,4096]{2,1,0:T(8,128)(2,1)} %down.43, bf16[10,64,512]{2,1,0:T(8,128)(2,1)S(1)} %copy-done.2), custom_call_target="tpu_custom_call" | custom-call | tf_op jit(solution)/shard_map/pick_step/pallas_call | solution.py:342
  37.6 13.7 %pick_step.22 = (bf16[16,4608]{1,0:T(8,128)(2,1)}, bf16[16,4608]{1,0:T(8,128)(2,1)}, bf16[16,4608]{1,0:T(8,128)(2,1)}) custom-call(s32[3]{0:T(128)} %pad_add_fusion.7.codes, bf16[10,64,4096]{2,1,0:T(8,128)(2,1)} %down.43, bf16[10,64,512]{2,1,0:T(8,128)(2,1)S(1)} %copy-done.2), custom_call_target="tpu_custom_call" | custom-call | tf_op jit(solution)/shard_map/pick_step/pallas_call | solution.py:342
  59.5 9.7 %pick_step.34 = (bf16[16,4608]{1,0:T(8,128)(2,1)}, bf16[16,4608]{1,0:T(8,128)(2,1)}, bf16[16,4608]{1,0:T(8,128)(2,1)}) custom-call(s32[3]{0:T(128)} %pad_add_fusion.8.codes, bf16[10,64,4096]{2,1,0:T(8,128)(2,1)} %down.43, bf16[10,64,512]{2,1,0:T(8,128)(2,1)S(1)} %copy-done.2, bf16[16,4608]{1,0:T(8,128)(2,1)S(1)} %collective-permute-done.32.refs_0_, ...), custom_call_target="tpu_custom_call" | custom-call | tf_op jit(solution)/shard_map/pick_step/pallas_call | solution.py:342
  75.9 9.7 %pick_step.23 = (bf16[16,4608]{1,0:T(8,128)(2,1)}, bf16[16,4608]{1,0:T(8,128)(2,1)}, bf16[16,4608]{1,0:T(8,128)(2,1)}) custom-call(s32[3]{0:T(128)} %pad_add_fusion.8.codes, bf16[10,64,4096]{2,1,0:T(8,128)(2,1)} %down.43, bf16[10,64,512]{2,1,0:T(8,128)(2,1)S(1)} %copy-done.2, bf16[16,4608]{1,0:T(8,128)(2,1)S(1)} %collective-permute-done.1.refs_0_, ...), custom_call_target="tpu_custom_call" | custom-call | tf_op jit(solution)/shard_map/pick_step/pallas_call | solution.py:342
  93.8 9.8 %pick_step.35 = (bf16[16,4608]{1,0:T(8,128)(2,1)}, bf16[16,4608]{1,0:T(8,128)(2,1)}, bf16[16,4608]{1,0:T(8,128)(2,1)}) custom-call(s32[3]{0:T(128)} %pad_add_fusion.9.codes, bf16[10,64,4096]{2,1,0:T(8,128)(2,1)} %down.43, bf16[10,64,512]{2,1,0:T(8,128)(2,1)S(1)} %copy-done.2, bf16[16,4608]{1,0:T(8,128)(2,1)S(1)} %collective-permute-done.32.refs_0_, ...), custom_call_target="tpu_custom_call" | custom-call | tf_op jit(solution)/shard_map/pick_step/pallas_call | solution.py:342
  110.2 9.8 %pick_step.24 = (bf16[16,4608]{1,0:T(8,128)(2,1)}, bf16[16,4608]{1,0:T(8,128)(2,1)}, bf16[16,4608]{1,0:T(8,128)(2,1)}) custom-call(s32[3]{0:T(128)} %pad_add_fusion.9.codes, bf16[10,64,4096]{2,1,0:T(8,128)(2,1)} %down.43, bf16[10,64,512]{2,1,0:T(8,128)(2,1)S(1)} %copy-done.2, bf16[16,4608]{1,0:T(8,128)(2,1)S(1)} %collective-permute-done.1.refs_0_, ...), custom_call_target="tpu_custom_call" | custom-call | tf_op jit(solution)/shard_map/pick_step/pallas_call | solution.py:342
  128.0 5.8 %pick_step.36 = (bf16[16,4608]{1,0:T(8,128)(2,1)}, bf16[16,4608]{1,0:T(8,128)(2,1)}, bf16[16,4608]{1,0:T(8,128)(2,1)}) custom-call(s32[3]{0:T(128)} %pad_add_fusion.10.codes, bf16[10,64,4096]{2,1,0:T(8,128)(2,1)} %down.43, bf16[10,64,512]{2,1,0:T(8,128)(2,1)S(1)} %copy-done.2, bf16[16,4608]{1,0:T(8,128)(2,1)S(1)} %collective-permute-done.32.refs_0_, ...), custom_call_target="tpu_custom_call" | custom-call | tf_op jit(solution)/shard_map/pick_step/pallas_call | solution.py:342
  139.9 5.8 %pick_step.25 = (bf16[16,4608]{1,0:T(8,128)(2,1)}, bf16[16,4608]{1,0:T(8,128)(2,1)}, bf16[16,4608]{1,0:T(8,128)(2,1)}) custom-call(s32[3]{0:T(128)} %pad_add_fusion.10.codes, bf16[10,64,4096]{2,1,0:T(8,128)(2,1)} %down.43, bf16[10,64,512]{2,1,0:T(8,128)(2,1)S(1)} %copy-done.2, bf16[16,4608]{1,0:T(8,128)(2,1)S(1)} %collective-permute-done.1.refs_0_, ...), custom_call_target="tpu_custom_call" | custom-call | tf_op jit(solution)/shard_map/pick_step/pallas_call | solution.py:342
  154.2 10.2 %pick_step.37 = (bf16[16,4608]{1,0:T(8,128)(2,1)}, bf16[16,4608]{1,0:T(8,128)(2,1)}, bf16[16,4608]{1,0:T(8,128)(2,1)}) custom-call(s32[3]{0:T(128)} %pad_add_fusion.11.codes, bf16[10,64,4096]{2,1,0:T(8,128)(2,1)} %down.43, bf16[10,64,512]{2,1,0:T(8,128)(2,1)S(1)} %copy-done.2, bf16[16,4608]{1,0:T(8,128)(2,1)S(1)} %collective-permute-done.32.refs_0_, ...), custom_call_target="tpu_custom_call" | custom-call | tf_op jit(solution)/shard_map/pick_step/pallas_call | solution.py:342
  171.9 10.3 %pick_step.26 = (bf16[16,4608]{1,0:T(8,128)(2,1)}, bf16[16,4608]{1,0:T(8,128)(2,1)}, bf16[16,4608]{1,0:T(8,128)(2,1)}) custom-call(s32[3]{0:T(128)} %pad_add_fusion.11.codes, bf16[10,64,4096]{2,1,0:T(8,128)(2,1)} %down.43, bf16[10,64,512]{2,1,0:T(8,128)(2,1)S(1)} %copy-done.2, bf16[16,4608]{1,0:T(8,128)(2,1)S(1)} %collective-permute-done.1.refs_0_, ...), custom_call_target="tpu_custom_call" | custom-call | tf_op jit(solution)/shard_map/pick_step/pallas_call | solution.py:342
  190.7 10.2 %pick_step.38 = (bf16[16,4608]{1,0:T(8,128)(2,1)}, bf16[16,4608]{1,0:T(8,128)(2,1)}, bf16[16,4608]{1,0:T(8,128)(2,1)}) custom-call(s32[3]{0:T(128)} %pad_add_fusion.12.codes, bf16[10,64,4096]{2,1,0:T(8,128)(2,1)} %down.43, bf16[10,64,512]{2,1,0:T(8,128)(2,1)S(1)} %copy-done.2, bf16[16,4608]{1,0:T(8,128)(2,1)S(1)} %collective-permute-done.32.refs_0_, ...), custom_call_target="tpu_custom_call" | custom-call | tf_op jit(solution)/shard_map/pick_step/pallas_call | solution.py:342
  208.4 10.3 %pick_step.27 = (bf16[16,4608]{1,0:T(8,128)(2,1)}, bf16[16,4608]{1,0:T(8,128)(2,1)}, bf16[16,4608]{1,0:T(8,128)(2,1)}) custom-call(s32[3]{0:T(128)} %pad_add_fusion.12.codes, bf16[10,64,4096]{2,1,0:T(8,128)(2,1)} %down.43, bf16[10,64,512]{2,1,0:T(8,128)(2,1)S(1)} %copy-done.2, bf16[16,4608]{1,0:T(8,128)(2,1)S(1)} %collective-permute-done.1.refs_0_, ...), custom_call_target="tpu_custom_call" | custom-call | tf_op jit(solution)/shard_map/pick_step/pallas_call | solution.py:342
  220.6 4.0 collective-permute-start.18
  228.6 6.4 %collective-permute-start.50 = (bf16[16,4608]{1,0:T(8,128)(2,1)}, bf16[16,4608]{1,0:T(8,128)(2,1)}, u32[]{:S(2)}, u32[]{:S(2)}) collective-permute-start(bf16[16,4608]{1,0:T(8,128)(2,1)} %get-tuple-element.337), channel_id=1, source_target_pairs={{0,2},{2,0},{4,6},{6,4},{8,10},{10,8},{12,14},{14,12},{1,3},{3,1},... | collective-permute-start | bytes 442376 | tf_op jit(solution)/shard_map/ppermute | solution.py:433
  236.9 4.0 collective-permute-start.52
  242.4 5.0 %collective-permute-start.19 = (bf16[16,4608]{1,0:T(8,128)(2,1)}, bf16[16,4608]{1,0:T(8,128)(2,1)}, u32[]{:S(2)}, u32[]{:S(2)}) collective-permute-start(bf16[16,4608]{1,0:T(8,128)(2,1)} %get-tuple-element.307), channel_id=1, source_target_pairs={{0,2},{2,0},{4,6},{6,4},{8,10},{10,8},{12,14},{14,12},{1,3},{3,1},... | collective-permute-start | bytes 442376 | tf_op jit(solution)/shard_map/ppermute | solution.py:433
  255.7 6.3 %pick_step.40 = (bf16[16,4608]{1,0:T(8,128)(2,1)}, bf16[16,4608]{1,0:T(8,128)(2,1)}, bf16[16,4608]{1,0:T(8,128)(2,1)}) custom-call(s32[3]{0:T(128)} %pad_add_fusion.14.codes, bf16[10,64,4096]{2,1,0:T(8,128)(2,1)} %down.43, bf16[10,64,512]{2,1,0:T(8,128)(2,1)S(1)} %copy-done.2, bf16[16,4608]{1,0:T(8,128)(2,1)S(1)} %collective-permute-done.32.refs_0_, ...), custom_call_target="tpu_custom_call" | custom-call | tf_op jit(solution)/shard_map/pick_step/pallas_call | solution.py:342
  264.0 4.0 collective-permute-start.55
  268.2 6.3 %pick_step.29 = (bf16[16,4608]{1,0:T(8,128)(2,1)}, bf16[16,4608]{1,0:T(8,128)(2,1)}, bf16[16,4608]{1,0:T(8,128)(2,1)}) custom-call(s32[3]{0:T(128)} %pad_add_fusion.14.codes, bf16[10,64,4096]{2,1,0:T(8,128)(2,1)} %down.43, bf16[10,64,512]{2,1,0:T(8,128)(2,1)S(1)} %copy-done.2, bf16[16,4608]{1,0:T(8,128)(2,1)S(1)} %collective-permute-done.1.refs_0_, ...), custom_call_target="tpu_custom_call" | custom-call | tf_op jit(solution)/shard_map/pick_step/pallas_call | solution.py:342
  277.9 4.2 collective-permute-start.24
  282.1 10.4 %fusion.10 = f32[1024,512]{1,0:T(8,128)} fusion(bf16[1024,4096]{1,0:T(8,128)(2,1)} %tokens.1, bf16[4096,1024]{1,0:T(8,128)(2,1)} %param.10, s32[]{:T(128)S(6)} %select_n.1332), kind=kOutput, calls=%fused_computation.17 | convolution fusion | flops 4294967296 | bytes 14680068 | tf_op jit(solution)/shard_map/dot_general | solution.py:458
  292.5 13.5 %collective-permute-start.64 = (f32[1024,512]{1,0:T(8,128)}, f32[1024,512]{1,0:T(8,128)S(1)}, u32[]{:S(2)}, u32[]{:S(2)}) collective-permute-start(f32[1024,512]{1,0:T(8,128)} %fusion.10), channel_id=1, source_target_pairs={{0,1},{1,0},{2,3},{3,2},{4,5},{5,4},{6,7},{7,6},{8,9},{9,8},{10,11... | collective-permute-start | bytes 6291464 | tf_op jit(solution)/shard_map/ppermute | solution.py:460
  308.5 10.8 %pick_step.41 = (bf16[16,4608]{1,0:T(8,128)(2,1)}, bf16[16,4608]{1,0:T(8,128)(2,1)}, bf16[16,4608]{1,0:T(8,128)(2,1)}) custom-call(s32[3]{0:T(128)} %pad_add_fusion.15.codes, bf16[10,64,4096]{2,1,0:T(8,128)(2,1)} %down.43, bf16[10,64,512]{2,1,0:T(8,128)(2,1)S(1)} %copy-done.2, bf16[16,4608]{1,0:T(8,128)(2,1)S(1)} %collective-permute-done.32.refs_0_, ...), custom_call_target="tpu_custom_call" | custom-call | tf_op jit(solution)/shard_map/pick_step/pallas_call | solution.py:342
  325.3 10.8 %pick_step.30 = (bf16[16,4608]{1,0:T(8,128)(2,1)}, bf16[16,4608]{1,0:T(8,128)(2,1)}, bf16[16,4608]{1,0:T(8,128)(2,1)}) custom-call(s32[3]{0:T(128)} %pad_add_fusion.15.codes, bf16[10,64,4096]{2,1,0:T(8,128)(2,1)} %down.43, bf16[10,64,512]{2,1,0:T(8,128)(2,1)S(1)} %copy-done.2, bf16[16,4608]{1,0:T(8,128)(2,1)S(1)} %collective-permute-done.1.refs_0_, ...), custom_call_target="tpu_custom_call" | custom-call | tf_op jit(solution)/shard_map/pick_step/pallas_call | solution.py:342
  344.6 6.4 %pick_step.42 = (bf16[16,4608]{1,0:T(8,128)(2,1)}, bf16[16,4608]{1,0:T(8,128)(2,1)}, bf16[16,4608]{1,0:T(8,128)(2,1)}) custom-call(s32[3]{0:T(128)} %pad_add_fusion.16.codes, bf16[10,64,4096]{2,1,0:T(8,128)(2,1)} %down.43, bf16[10,64,512]{2,1,0:T(8,128)(2,1)S(1)} %copy-done.2, bf16[16,4608]{1,0:T(8,128)(2,1)S(1)} %collective-permute-done.32.refs_0_, ...), custom_call_target="tpu_custom_call" | custom-call | tf_op jit(solution)/shard_map/pick_step/pallas_call | solution.py:342
  354.6 4.0 collective-permute-start.61
  358.7 6.4 %pick_step.31 = (bf16[16,4608]{1,0:T(8,128)(2,1)}, bf16[16,4608]{1,0:T(8,128)(2,1)}, bf16[16,4608]{1,0:T(8,128)(2,1)}) custom-call(s32[3]{0:T(128)} %pad_add_fusion.16.codes, bf16[10,64,4096]{2,1,0:T(8,128)(2,1)} %down.43, bf16[10,64,512]{2,1,0:T(8,128)(2,1)S(1)} %copy-done.2, bf16[16,4608]{1,0:T(8,128)(2,1)S(1)} %collective-permute-done.1.refs_0_, ...), custom_call_target="tpu_custom_call" | custom-call | tf_op jit(solution)/shard_map/pick_step/pallas_call | solution.py:342
  379.4 72.0 %conditional.1 = (bf16[4,64,4608]{2,1,0:T(8,128)(2,1)}) conditional(s32[]{:T(128)} %bitcast.11, (s32[8,4]{1,0:T(8,128)S(1)}, s32[]{:T(128)}, bf16[10,64,4096]{2,1,0:T(8,128)(2,1)}, bf16[10,64,512]{2,1,0:T(8,128)(2,1)S(1)}) %tuple.89, (s32[32,2]{0,1:T(2,128)S(1)}, s32[]{:T(128)}, pred[]{:T(512)}, bf16[10,64,4096]{2,1,0:T(8,128)(2,1)}, ...), branch_computations={%region_25.27_spmd, %region_27.28_spmd} | conditional | flops 1499 | bytes 18878898 | solution.py:442
  380.1 71.3 %collect.1 = bf16[4,64,4608]{2,1,0:T(8,128)(2,1)} custom-call(s32[8]{0:T(128)} %dynamic-slice_bitcast_fusion.codes, bf16[10,64,4096]{2,1,0:T(8,128)(2,1)} %get-tuple-element.165.down, bf16[10,64,512]{2,1,0:T(8,128)(2,1)S(1)} %get-tuple-element.166.up, bf16[16,4608]{1,0:T(8,128)(2,1)S(1)} %get-tuple-element.167.refs_0_, ...), custom_call_target="tpu_custom_call" | custom-call | tf_op jit(solution)/shard_map/cond/branch_1_fun/collect/pallas_call | solution.py:387
  454.8 6.4 %codes.1.refs_0_ = f32[1024,64]{1,0:T(8,128)S(1)} custom-call(s32[4]{0:T(128)S(1)} %iota.214.place, s32[4]{0:T(128)S(1)} %bitcast.78, bf16[1024,4096]{1,0:T(8,128)(2,1)S(1)} %copy-done.1, bf16[4,64,4608]{2,1,0:T(8,128)(2,1)} %get-tuple-element.655.refs_0_.refs_1_.refs_2_.refs_3_.refs_4_.refs_5_.refs_6_.refs_7_, ...), custom_call_target="tpu_custom_call" | custom-call | tf_op jit(solution)/shard_map/codes/pallas_call | solution.py:73
  461.2 5.2 %collective-permute-start.63 = (f32[1024,64]{1,0:T(8,128)S(1)}, f32[1024,64]{1,0:T(8,128)S(1)}, u32[]{:S(2)}, u32[]{:S(2)}) collective-permute-start(f32[1024,64]{1,0:T(8,128)S(1)} %codes.1.refs_0_), channel_id=1, source_target_pairs={{0,1},{1,0},{2,3},{3,2},{4,5},{5,4},{6,7},{7,6},{8,9},{9,8},{10,11... | collective-permute-start | bytes 786440 | tf_op jit(solution)/shard_map/ppermute | solution.py:154
  466.4 6.5 %fusion.7.refs_2_ = f32[1024,512]{1,0:T(8,128)S(1)} fusion(bf16[1024,4096]{1,0:T(8,128)(2,1)S(1)} %copy-done.1, bf16[4096,1024]{1,0:T(8,128)(2,1)} %param.10, s32[]{:T(128)S(6)} %select_n.1331), kind=kOutput, calls=%fused_computation.16 | convolution fusion | flops 4294967296 | bytes 14680068 | tf_op jit(solution)/shard_map/dot_general | solution.py:458
  (288 shorter events, 161.0 us)
Async XLA Ops:
  31.0 23.8 %collective-permute-start.32 = (bf16[16,4608]{1,0:T(8,128)(2,1)}, bf16[16,4608]{1,0:T(8,128)(2,1)S(1)}, u32[]{:S(2)}, u32[]{:S(2)}) collective-permute-start(bf16[16,4608]{1,0:T(8,128)(2,1)} %get-tuple-element.319), channel_id=1, source_target_pairs={{0,2},{2,0},{4,6},{6,4},{8,10},{10,8},{12,14},{14,12},{1,3},{3,1},... | collective-permute-start | bytes 442376 | tf_op jit(solution)/shard_map/ppermute | solution.py:433
  32.3 27.2 %collective-permute-start.33 = (bf16[16,4608]{1,0:T(8,128)(2,1)}, bf16[16,4608]{1,0:T(8,128)(2,1)S(1)}, u32[]{:S(2)}, u32[]{:S(2)}) collective-permute-start(bf16[16,4608]{1,0:T(8,128)(2,1)} %get-tuple-element.320), channel_id=1, source_target_pairs={{0,4},{2,6},{4,8},{6,10},{8,12},{10,14},{1,5},{3,7},{5,9},{7,11},{... | collective-permute-start | bytes 442376 | tf_op jit(solution)/shard_map/ppermute | solution.py:433
  35.5 24.1 %collective-permute-start.34 = (bf16[16,4608]{1,0:T(8,128)(2,1)}, bf16[16,4608]{1,0:T(8,128)(2,1)S(1)}, u32[]{:S(2)}, u32[]{:S(2)}) collective-permute-start(bf16[16,4608]{1,0:T(8,128)(2,1)} %get-tuple-element.321), channel_id=1, source_target_pairs={{4,0},{6,2},{8,4},{10,6},{12,8},{14,10},{5,1},{7,3},{9,5},{11,7},{... | collective-permute-start | bytes 442376 | tf_op jit(solution)/shard_map/ppermute | solution.py:433
  51.3 22.5 %collective-permute-start.1 = (bf16[16,4608]{1,0:T(8,128)(2,1)}, bf16[16,4608]{1,0:T(8,128)(2,1)S(1)}, u32[]{:S(2)}, u32[]{:S(2)}) collective-permute-start(bf16[16,4608]{1,0:T(8,128)(2,1)} %get-tuple-element.289), channel_id=1, source_target_pairs={{0,2},{2,0},{4,6},{6,4},{8,10},{10,8},{12,14},{14,12},{1,3},{3,1},... | collective-permute-start | bytes 442376 | tf_op jit(solution)/shard_map/ppermute | solution.py:433
  51.6 24.2 %collective-permute-start.2 = (bf16[16,4608]{1,0:T(8,128)(2,1)}, bf16[16,4608]{1,0:T(8,128)(2,1)S(1)}, u32[]{:S(2)}, u32[]{:S(2)}) collective-permute-start(bf16[16,4608]{1,0:T(8,128)(2,1)} %get-tuple-element.290), channel_id=1, source_target_pairs={{0,4},{2,6},{4,8},{6,10},{8,12},{10,14},{1,5},{3,7},{5,9},{7,11},{... | collective-permute-start | bytes 442376 | tf_op jit(solution)/shard_map/ppermute | solution.py:433
  54.8 21.1 %collective-permute-start.3 = (bf16[16,4608]{1,0:T(8,128)(2,1)}, bf16[16,4608]{1,0:T(8,128)(2,1)S(1)}, u32[]{:S(2)}, u32[]{:S(2)}) collective-permute-start(bf16[16,4608]{1,0:T(8,128)(2,1)} %get-tuple-element.291), channel_id=1, source_target_pairs={{4,0},{6,2},{8,4},{10,6},{12,8},{14,10},{5,1},{7,3},{9,5},{11,7},{... | collective-permute-start | bytes 442376 | tf_op jit(solution)/shard_map/ppermute | solution.py:433
  70.6 23.2 %collective-permute-start.36 = (bf16[16,4608]{1,0:T(8,128)(2,1)}, bf16[16,4608]{1,0:T(8,128)(2,1)S(1)}, u32[]{:S(2)}, u32[]{:S(2)}) collective-permute-start(bf16[16,4608]{1,0:T(8,128)(2,1)} %get-tuple-element.323), channel_id=1, source_target_pairs={{0,4},{2,6},{4,8},{6,10},{8,12},{10,14},{1,5},{3,7},{5,9},{7,11},{... | collective-permute-start | bytes 442376 | tf_op jit(solution)/shard_map/ppermute | solution.py:433
  85.6 21.1 %collective-permute-start.4 = (bf16[16,4608]{1,0:T(8,128)(2,1)}, bf16[16,4608]{1,0:T(8,128)(2,1)S(1)}, u32[]{:S(2)}, u32[]{:S(2)}) collective-permute-start(bf16[16,4608]{1,0:T(8,128)(2,1)} %get-tuple-element.292), channel_id=1, source_target_pairs={{0,2},{2,0},{4,6},{6,4},{8,10},{10,8},{12,14},{14,12},{1,3},{3,1},... | collective-permute-start | bytes 442376 | tf_op jit(solution)/shard_map/ppermute | solution.py:433
  86.0 24.2 %collective-permute-start.5 = (bf16[16,4608]{1,0:T(8,128)(2,1)}, bf16[16,4608]{1,0:T(8,128)(2,1)S(1)}, u32[]{:S(2)}, u32[]{:S(2)}) collective-permute-start(bf16[16,4608]{1,0:T(8,128)(2,1)} %get-tuple-element.293), channel_id=1, source_target_pairs={{0,4},{2,6},{4,8},{6,10},{8,12},{10,14},{1,5},{3,7},{5,9},{7,11},{... | collective-permute-start | bytes 442376 | tf_op jit(solution)/shard_map/ppermute | solution.py:433
  89.2 21.0 %collective-permute-start.6 = (bf16[16,4608]{1,0:T(8,128)(2,1)}, bf16[16,4608]{1,0:T(8,128)(2,1)S(1)}, u32[]{:S(2)}, u32[]{:S(2)}) collective-permute-start(bf16[16,4608]{1,0:T(8,128)(2,1)} %get-tuple-element.294), channel_id=1, source_target_pairs={{4,0},{6,2},{8,4},{10,6},{12,8},{14,10},{5,1},{7,3},{9,5},{11,7},{... | collective-permute-start | bytes 442376 | tf_op jit(solution)/shard_map/ppermute | solution.py:433
  104.8 23.2 %collective-permute-start.39 = (bf16[16,4608]{1,0:T(8,128)(2,1)}, bf16[16,4608]{1,0:T(8,128)(2,1)S(1)}, u32[]{:S(2)}, u32[]{:S(2)}) collective-permute-start(bf16[16,4608]{1,0:T(8,128)(2,1)} %get-tuple-element.326), channel_id=1, source_target_pairs={{0,4},{2,6},{4,8},{6,10},{8,12},{10,14},{1,5},{3,7},{5,9},{7,11},{... | collective-permute-start | bytes 442376 | tf_op jit(solution)/shard_map/ppermute | solution.py:433
  106.7 21.2 %collective-permute-start.40 = (bf16[16,4608]{1,0:T(8,128)(2,1)}, bf16[16,4608]{1,0:T(8,128)(2,1)S(1)}, u32[]{:S(2)}, u32[]{:S(2)}) collective-permute-start(bf16[16,4608]{1,0:T(8,128)(2,1)} %get-tuple-element.327), channel_id=1, source_target_pairs={{4,0},{6,2},{8,4},{10,6},{12,8},{14,10},{5,1},{7,3},{9,5},{11,7},{... | collective-permute-start | bytes 442376 | tf_op jit(solution)/shard_map/ppermute | solution.py:433
  145.7 22.2 %collective-permute-start.10 = (bf16[16,4608]{1,0:T(8,128)(2,1)}, bf16[16,4608]{1,0:T(8,128)(2,1)}, u32[]{:S(2)}, u32[]{:S(2)}) collective-permute-start(bf16[16,4608]{1,0:T(8,128)(2,1)} %get-tuple-element.298), channel_id=1, source_target_pairs={{0,2},{2,0},{4,6},{6,4},{8,10},{10,8},{12,14},{14,12},{1,3},{3,1},... | collective-permute-start | bytes 442376 | tf_op jit(solution)/shard_map/ppermute | solution.py:433
  145.7 26.1 %collective-permute-start.11 = (bf16[16,4608]{1,0:T(8,128)(2,1)}, bf16[16,4608]{1,0:T(8,128)(2,1)}, u32[]{:S(2)}, u32[]{:S(2)}) collective-permute-start(bf16[16,4608]{1,0:T(8,128)(2,1)} %get-tuple-element.299), channel_id=1, source_target_pairs={{0,4},{2,6},{4,8},{6,10},{8,12},{10,14},{1,5},{3,7},{5,9},{7,11},{... | collective-permute-start | bytes 442376 | tf_op jit(solution)/shard_map/ppermute | solution.py:433
  147.7 24.2 %collective-permute-start.12 = (bf16[16,4608]{1,0:T(8,128)(2,1)}, bf16[16,4608]{1,0:T(8,128)(2,1)}, u32[]{:S(2)}, u32[]{:S(2)}) collective-permute-start(bf16[16,4608]{1,0:T(8,128)(2,1)} %get-tuple-element.300), channel_id=1, source_target_pairs={{4,0},{6,2},{8,4},{10,6},{12,8},{14,10},{5,1},{7,3},{9,5},{11,7},{... | collective-permute-start | bytes 442376 | tf_op jit(solution)/shard_map/ppermute | solution.py:433
  165.9 24.7 %collective-permute-start.45 = (bf16[16,4608]{1,0:T(8,128)(2,1)}, bf16[16,4608]{1,0:T(8,128)(2,1)}, u32[]{:S(2)}, u32[]{:S(2)}) collective-permute-start(bf16[16,4608]{1,0:T(8,128)(2,1)} %get-tuple-element.332), channel_id=1, source_target_pairs={{0,4},{2,6},{4,8},{6,10},{8,12},{10,14},{1,5},{3,7},{5,9},{7,11},{... | collective-permute-start | bytes 442376 | tf_op jit(solution)/shard_map/ppermute | solution.py:433
  167.9 22.8 %collective-permute-start.46 = (bf16[16,4608]{1,0:T(8,128)(2,1)}, bf16[16,4608]{1,0:T(8,128)(2,1)}, u32[]{:S(2)}, u32[]{:S(2)}) collective-permute-start(bf16[16,4608]{1,0:T(8,128)(2,1)} %get-tuple-element.333), channel_id=1, source_target_pairs={{4,0},{6,2},{8,4},{10,6},{12,8},{14,10},{5,1},{7,3},{9,5},{11,7},{... | collective-permute-start | bytes 442376 | tf_op jit(solution)/shard_map/ppermute | solution.py:433
  182.2 22.2 %collective-permute-start.13 = (bf16[16,4608]{1,0:T(8,128)(2,1)}, bf16[16,4608]{1,0:T(8,128)(2,1)}, u32[]{:S(2)}, u32[]{:S(2)}) collective-permute-start(bf16[16,4608]{1,0:T(8,128)(2,1)} %get-tuple-element.301), channel_id=1, source_target_pairs={{0,2},{2,0},{4,6},{6,4},{8,10},{10,8},{12,14},{14,12},{1,3},{3,1},... | collective-permute-start | bytes 442376 | tf_op jit(solution)/shard_map/ppermute | solution.py:433
  182.3 26.1 %collective-permute-start.14 = (bf16[16,4608]{1,0:T(8,128)(2,1)}, bf16[16,4608]{1,0:T(8,128)(2,1)}, u32[]{:S(2)}, u32[]{:S(2)}) collective-permute-start(bf16[16,4608]{1,0:T(8,128)(2,1)} %get-tuple-element.302), channel_id=1, source_target_pairs={{0,4},{2,6},{4,8},{6,10},{8,12},{10,14},{1,5},{3,7},{5,9},{7,11},{... | collective-permute-start | bytes 442376 | tf_op jit(solution)/shard_map/ppermute | solution.py:433
  184.2 24.2 %collective-permute-start.15 = (bf16[16,4608]{1,0:T(8,128)(2,1)}, bf16[16,4608]{1,0:T(8,128)(2,1)}, u32[]{:S(2)}, u32[]{:S(2)}) collective-permute-start(bf16[16,4608]{1,0:T(8,128)(2,1)} %get-tuple-element.303), channel_id=1, source_target_pairs={{4,0},{6,2},{8,4},{10,6},{12,8},{14,10},{5,1},{7,3},{9,5},{11,7},{... | collective-permute-start | bytes 442376 | tf_op jit(solution)/shard_map/ppermute | solution.py:433
  202.4 24.7 %collective-permute-start.48 = (bf16[16,4608]{1,0:T(8,128)(2,1)}, bf16[16,4608]{1,0:T(8,128)(2,1)}, u32[]{:S(2)}, u32[]{:S(2)}) collective-permute-start(bf16[16,4608]{1,0:T(8,128)(2,1)} %get-tuple-element.335), channel_id=1, source_target_pairs={{0,4},{2,6},{4,8},{6,10},{8,12},{10,14},{1,5},{3,7},{5,9},{7,11},{... | collective-permute-start | bytes 442376 | tf_op jit(solution)/shard_map/ppermute | solution.py:433
  204.3 22.8 %collective-permute-start.49 = (bf16[16,4608]{1,0:T(8,128)(2,1)}, bf16[16,4608]{1,0:T(8,128)(2,1)}, u32[]{:S(2)}, u32[]{:S(2)}) collective-permute-start(bf16[16,4608]{1,0:T(8,128)(2,1)} %get-tuple-element.336), channel_id=1, source_target_pairs={{4,0},{6,2},{8,4},{10,6},{12,8},{14,10},{5,1},{7,3},{9,5},{11,7},{... | collective-permute-start | bytes 442376 | tf_op jit(solution)/shard_map/ppermute | solution.py:433
  218.7 22.2 %collective-permute-start.17 = (bf16[16,4608]{1,0:T(8,128)(2,1)}, bf16[16,4608]{1,0:T(8,128)(2,1)}, u32[]{:S(2)}, u32[]{:S(2)}) collective-permute-start(bf16[16,4608]{1,0:T(8,128)(2,1)} %get-tuple-element.305), channel_id=1, source_target_pairs={{0,4},{2,6},{4,8},{6,10},{8,12},{10,14},{1,5},{3,7},{5,9},{7,11},{... | collective-permute-start | bytes 442376 | tf_op jit(solution)/shard_map/ppermute | solution.py:433
  242.4 21.7 %collective-permute-start.19 = (bf16[16,4608]{1,0:T(8,128)(2,1)}, bf16[16,4608]{1,0:T(8,128)(2,1)}, u32[]{:S(2)}, u32[]{:S(2)}) collective-permute-start(bf16[16,4608]{1,0:T(8,128)(2,1)} %get-tuple-element.307), channel_id=1, source_target_pairs={{0,2},{2,0},{4,6},{6,4},{8,10},{10,8},{12,14},{14,12},{1,3},{3,1},... | collective-permute-start | bytes 442376 | tf_op jit(solution)/shard_map/ppermute | solution.py:433
  262.1 30.4 %collective-permute-start.54 = (bf16[16,4608]{1,0:T(8,128)(2,1)}, bf16[16,4608]{1,0:T(8,128)(2,1)}, u32[]{:S(2)}, u32[]{:S(2)}) collective-permute-start(bf16[16,4608]{1,0:T(8,128)(2,1)} %get-tuple-element.341), channel_id=1, source_target_pairs={{0,4},{2,6},{4,8},{6,10},{8,12},{10,14},{1,5},{3,7},{5,9},{7,11},{... | collective-permute-start | bytes 442376 | tf_op jit(solution)/shard_map/ppermute | solution.py:433
  264.0 44.5 %collective-permute-start.55 = (bf16[16,4608]{1,0:T(8,128)(2,1)}, bf16[16,4608]{1,0:T(8,128)(2,1)}, u32[]{:S(2)}, u32[]{:S(2)}) collective-permute-start(bf16[16,4608]{1,0:T(8,128)(2,1)} %get-tuple-element.342), channel_id=1, source_target_pairs={{4,0},{6,2},{8,4},{10,6},{12,8},{14,10},{5,1},{7,3},{9,5},{11,7},{... | collective-permute-start | bytes 442376 | tf_op jit(solution)/shard_map/ppermute | solution.py:433
  274.5 44.9 %collective-permute-start.22 = (bf16[16,4608]{1,0:T(8,128)(2,1)}, bf16[16,4608]{1,0:T(8,128)(2,1)}, u32[]{:S(2)}, u32[]{:S(2)}) collective-permute-start(bf16[16,4608]{1,0:T(8,128)(2,1)} %get-tuple-element.310), channel_id=1, source_target_pairs={{0,2},{2,0},{4,6},{6,4},{8,10},{10,8},{12,14},{14,12},{1,3},{3,1},... | collective-permute-start | bytes 442376 | tf_op jit(solution)/shard_map/ppermute | solution.py:433
  276.0 45.3 %collective-permute-start.23 = (bf16[16,4608]{1,0:T(8,128)(2,1)}, bf16[16,4608]{1,0:T(8,128)(2,1)}, u32[]{:S(2)}, u32[]{:S(2)}) collective-permute-start(bf16[16,4608]{1,0:T(8,128)(2,1)} %get-tuple-element.311), channel_id=1, source_target_pairs={{0,4},{2,6},{4,8},{6,10},{8,12},{10,14},{1,5},{3,7},{5,9},{7,11},{... | collective-permute-start | bytes 442376 | tf_op jit(solution)/shard_map/ppermute | solution.py:433
  277.9 47.4 %collective-permute-start.24 = (bf16[16,4608]{1,0:T(8,128)(2,1)}, bf16[16,4608]{1,0:T(8,128)(2,1)}, u32[]{:S(2)}, u32[]{:S(2)}) collective-permute-start(bf16[16,4608]{1,0:T(8,128)(2,1)} %get-tuple-element.312), channel_id=1, source_target_pairs={{4,0},{6,2},{8,4},{10,6},{12,8},{14,10},{5,1},{7,3},{9,5},{11,7},{... | collective-permute-start | bytes 442376 | tf_op jit(solution)/shard_map/ppermute | solution.py:433
  292.5 180.5 %collective-permute-start.64 = (f32[1024,512]{1,0:T(8,128)}, f32[1024,512]{1,0:T(8,128)S(1)}, u32[]{:S(2)}, u32[]{:S(2)}) collective-permute-start(f32[1024,512]{1,0:T(8,128)} %fusion.10), channel_id=1, source_target_pairs={{0,1},{1,0},{2,3},{3,2},{4,5},{5,4},{6,7},{7,6},{8,9},{9,8},{10,11... | collective-permute-start | bytes 6291464 | tf_op jit(solution)/shard_map/ppermute | solution.py:460
  319.4 21.2 %collective-permute-start.57 = (bf16[16,4608]{1,0:T(8,128)(2,1)}, bf16[16,4608]{1,0:T(8,128)(2,1)}, u32[]{:S(2)}, u32[]{:S(2)}) collective-permute-start(bf16[16,4608]{1,0:T(8,128)(2,1)} %get-tuple-element.344), channel_id=1, source_target_pairs={{0,4},{2,6},{4,8},{6,10},{8,12},{10,14},{1,5},{3,7},{5,9},{7,11},{... | collective-permute-start | bytes 442376 | tf_op jit(solution)/shard_map/ppermute | solution.py:433
  321.3 23.2 %collective-permute-start.58 = (bf16[16,4608]{1,0:T(8,128)(2,1)}, bf16[16,4608]{1,0:T(8,128)(2,1)}, u32[]{:S(2)}, u32[]{:S(2)}) collective-permute-start(bf16[16,4608]{1,0:T(8,128)(2,1)} %get-tuple-element.345), channel_id=1, source_target_pairs={{4,0},{6,2},{8,4},{10,6},{12,8},{14,10},{5,1},{7,3},{9,5},{11,7},{... | collective-permute-start | bytes 442376 | tf_op jit(solution)/shard_map/ppermute | solution.py:433
  (53 other events, 2618.9 us)

commit v3 on v1

v3 whole, which is shorter than its diff:
```python
import functools

import jax
import jax.numpy as jnp
from jax import lax
from jax.experimental import pallas as pl
from jax.experimental.pallas import tpu as pltpu
from jax.sharding import PartitionSpec as P

ADAPTER_SCALE = 2.0
MIB = 1 << 20
ANY = pl.BlockSpec(memory_space=pl.ANY)
VMEM = pl.BlockSpec(memory_space=pltpu.VMEM)


def in_hbm(x):
    return pltpu.with_memory_space_constraint(x, pltpu.HBM)


def pick_kernel(rows, req, ids, owner_map, down, up, out, wanted, sem):
    held, _, width = down.shape
    first = lax.axis_index("dp") * held

    def fetch(j, carry):
        wanted[j] = 0
        for r in range(req):
            slot = owner_map[ids[j * req + r]] - first

            @pl.when((slot >= 0) & (slot < held))
            def _(slot=slot):
                wanted[j] = 1
                to = out.at[j]
                pltpu.make_async_copy(down.at[slot], to.at[:, pl.ds(0, width)], sem.at[j]).start()
                pltpu.make_async_copy(
                    up.at[slot], to.at[:, pl.ds(width, up.shape[2])], sem.at[j]
                ).start()

        return carry

    def drain(j, carry):
        @pl.when(wanted[j] == 1)
        def _():
            pltpu.make_async_copy(out.at[j], out.at[j], sem.at[j]).wait()

        return carry

    for body in (fetch, drain):
        lax.fori_loop(0, rows, body, 0)


def pick(adapter_ids, owner_map, down_pool, up_pool):
    rows, req = adapter_ids.shape
    rank, width = down_pool.shape[1:]
    wide = width + up_pool.shape[2]
    return pl.pallas_call(
        functools.partial(pick_kernel, rows, req),
        grid_spec=pltpu.PrefetchScalarGridSpec(
            num_scalar_prefetch=2,
            grid=(),
            in_specs=[ANY, ANY],
            out_specs=ANY,
            scratch_shapes=[
                pltpu.SMEM((rows,), jnp.int32),
                pltpu.SemaphoreType.DMA((rows,)),
            ],
        ),
        out_shape=pltpu.VMEM((rows, rank, wide), down_pool.dtype),
        compiler_params=pltpu.CompilerParams(vmem_limit_bytes=24 * MIB),
        name="pick",
    )(adapter_ids.reshape(-1), owner_map, in_hbm(down_pool), in_hbm(up_pool))


def stage_kernel(source, out, sem):
    copy = pltpu.make_async_copy(source, out, sem)
    copy.start()
    copy.wait()


def stage(x):
    return pl.pallas_call(
        stage_kernel,
        in_specs=[ANY],
        out_specs=VMEM,
        out_shape=pltpu.VMEM(x.shape, x.dtype),
        scratch_shapes=[pltpu.SemaphoreType.DMA],
        compiler_params=pltpu.CompilerParams(vmem_limit_bytes=24 * MIB),
        cost_estimate=pl.CostEstimate(flops=0, bytes_accessed=2 * x.size * x.dtype.itemsize, transcendentals=0),
        name="stage",
    )(in_hbm(x))


def request_of_rows(ends, count, first, rows):
    at = first + lax.broadcasted_iota(jnp.int32, (rows, 1), 0)
    which = jnp.zeros((rows, 1), jnp.int32)
    for r in range(count - 1):
        which += (at >= ends[r]).astype(jnp.int32)
    return which


def code_kernel(count, tile, place, ends, tokens, blocks, out, down, sem):
    rank, width = blocks.shape[1], tokens.shape[1]
    for r in range(count):
        pltpu.make_async_copy(
            blocks.at[place[r], :, pl.ds(0, width)], down.at[pl.ds(r * rank, rank), :], sem
        ).start()
    pltpu.make_async_copy(down, down, sem).wait()
    for i in range(out.shape[0] // tile):
        parts = []
        for side in range(2):
            first = side * out.shape[0] + i * tile
            full = lax.dot_general(
                tokens[first : first + tile, :],
                down[...],
                (((1,), (1,)), ((), ())),
                preferred_element_type=jnp.float32,
            )
            which = request_of_rows(ends, count, first, tile)
            code = jnp.zeros((tile, rank), jnp.float32)
            for r in range(count):
                code = jnp.where(which == r, full[:, r * rank : (r + 1) * rank], code)
            parts.append(code)
        out[i * tile : (i + 1) * tile, :] = jnp.concatenate(parts, axis=1)


def codes(place, ends, tokens, blocks):
    many, features = tokens.shape
    count = place.shape[0]
    rank = blocks.shape[1]
    return pl.pallas_call(
        functools.partial(code_kernel, count, min(256, many // 2)),
        grid_spec=pltpu.PrefetchScalarGridSpec(
            num_scalar_prefetch=2,
            grid=(),
            in_specs=[VMEM, ANY],
            out_specs=VMEM,
            scratch_shapes=[
                pltpu.VMEM((count * rank, features), blocks.dtype),
                pltpu.SemaphoreType.DMA,
            ],
        ),
        out_shape=jax.ShapeDtypeStruct((many // 2, 2 * rank), jnp.float32),
        compiler_params=pltpu.CompilerParams(vmem_limit_bytes=32 * MIB),
        cost_estimate=pl.CostEstimate(
            flops=2 * many * features * count * rank,
            bytes_accessed=count * rank * features * 2,
            transcendentals=0,
        ),
        name="codes",
    )(place, ends, pltpu.with_memory_space_constraint(tokens, pltpu.VMEM), blocks)


def finish_kernel(count, parts, place, ends, *refs):
    code_parts, base = refs[:parts], refs[parts]
    blocks = refs[parts + 1 : parts + 1 + count]
    out, up = refs[parts + 1 + count :]
    rank = blocks[0].shape[1]
    step = pl.program_id(0)

    @pl.when(step == 0)
    def _():
        for r in range(count):
            up[r * rank : (r + 1) * rank, :] = blocks[r][0]

    rows = out.shape[0]
    code = code_parts[0][...]
    for p in range(1, parts):
        code = code + code_parts[p][...]
    code = jnp.where(step < pl.num_programs(0) // 2, code[:, :rank], code[:, rank:])
    which = request_of_rows(ends, count, step * rows, rows)
    zero = jnp.zeros_like(code)
    wide = jnp.concatenate([jnp.where(which == r, code, zero) for r in range(count)], axis=1)
    delta = None
    for _ in range(3):
        part = wide.astype(jnp.bfloat16)
        wide = wide - part.astype(jnp.float32)
        term = jnp.dot(part, up[...], preferred_element_type=jnp.float32)
        delta = term if delta is None else delta + term
    out[...] = (base[...] + ADAPTER_SCALE * delta).astype(out.dtype)


def finish(place, ends, code_parts, base, blocks, width):
    many, columns = base.shape
    rank = blocks.shape[1]
    count = place.shape[0]
    parts = len(code_parts)
    tile = min(256, many // 2)
    half = many // tile // 2
    return pl.pallas_call(
        functools.partial(finish_kernel, count, parts),
        grid_spec=pltpu.PrefetchScalarGridSpec(
            num_scalar_prefetch=2,
            grid=(many // tile,),
            in_specs=[pl.BlockSpec((tile, 2 * rank), lambda i, place, ends: (i % half, 0))] * parts
            + [pl.BlockSpec((tile, columns), lambda i, place, ends: (i, 0))]
            + [
                pl.BlockSpec(
                    (1, rank, columns),
                    lambda i, place, ends, r=r: (place[r], 0, width // columns),
                )
                for r in range(count)
            ],
            out_specs=pl.BlockSpec((tile, columns), lambda i, place, ends: (i, 0)),
            scratch_shapes=[pltpu.VMEM((count * rank, columns), blocks.dtype)],
        ),
        out_shape=jax.ShapeDtypeStruct((many, columns), jnp.bfloat16),
        compiler_params=pltpu.CompilerParams(vmem_limit_bytes=24 * MIB),
        name="finish",
    )(place, ends, *code_parts, base, *([blocks] * count))


def gathered(part, axis, size):
    held = [part]
    for step in range(1, size):
        held.append(lax.ppermute(part, axis, [(i, (i + step) % size) for i in range(size)]))
    return held


def shards(sizes, tokens, key_weight, down_pool, up_pool, adapter_ids, lengths, owner_map):
    n_groups, n_dp, n_tensor = sizes
    held, _, width = down_pool.shape
    columns = up_pool.shape[2]

    send = pick(adapter_ids, owner_map, down_pool, up_pool)
    send, late_tokens = lax.optimization_barrier((send, tokens))
    blocks = lax.all_to_all(send, "dp", split_axis=0, concat_axis=0, tiled=True)

    me = lax.axis_index("tensor")
    base = None
    for step in reversed(range(n_tensor)):
        to = lax.rem(me + step, n_tensor)
        weight = lax.dynamic_slice_in_dim(key_weight, to * columns, columns, 1)
        part = jnp.dot(late_tokens, weight, preferred_element_type=jnp.float32)
        if step:
            part = lax.ppermute(
                part, "tensor", [(i, (i + step) % n_tensor) for i in range(n_tensor)]
            )
        base = part if base is None else base + part
    at_hand = stage(late_tokens)
    my_ids = lax.dynamic_index_in_dim(adapter_ids, lax.axis_index("dp"), 0, keepdims=False)
    place = owner_map[my_ids] // held
    ends = jnp.cumsum(lengths[0]).astype(jnp.int32)

    blocks, base, at_hand, place, ends = lax.optimization_barrier(
        (blocks, base, at_hand, place, ends)
    )
    code = codes(place, ends, at_hand, blocks)
    code_parts = gathered(code, "tensor", n_tensor)
    return finish(place, ends, code_parts, base, blocks, width)


def solution(mesh):
    placed = (
        P(("groups", "dp"), "tensor"),
        P("tensor", None),
        P("dp", None, "tensor"),
        P("dp", None, "tensor"),
        P("groups", None),
        P(("groups", "dp"), None),
        P("groups"),
    )
    sizes = tuple(mesh.shape[name] for name in ("groups", "dp", "tensor"))
    return jax.shard_map(
        functools.partial(shards, sizes),
        mesh=mesh,
        in_specs=placed,
        out_specs=P(("groups", "dp"), "tensor"),
        check_vma=False,
    )
```

time: 142 us -> 132 us (0.930)
  the two profiles are of different devices: /device:TPU:1 before, /device:TPU:0 now
where the time goes in v3:
time: 132 us
  waiting for transfers between devices  80.3 us (61%)
  matrix products  17.9 us (14%)
  Pallas kernels  15.1 us (11%)
  local copies, waits for them, and re-layouts  11 us (8%)
  starting transfers between devices  7.62 us (6%)
    all_to_all x1, waiting for transfers between devices, shards(): blocks = lax.all_to_all(send, 'dp', split_axis=0, concat_axis=0, tiled=True)  78.8 us
    dot_general x2, matrix products, shards(): part = jnp.dot(late_tokens, weight, preferred_element_type=jnp.float32)  17.9 us
    unnamed x15, local copies, waits for them, and re-layouts  10.1 us
    all_to_all x1, starting transfers between devices, shards(): blocks = lax.all_to_all(send, 'dp', split_axis=0, concat_axis=0, tiled=True)  7.47 us
    pallas_call x1, Pallas kernels, codes(): pl.pallas_call(functools.partial(code_kernel, count, min(256, many // 2))...  4.73 us
    pallas_call x1, Pallas kernels, finish(): pl.pallas_call(functools.partial(finish_kernel, count, parts), grid_spec=...  4.5 us
    pallas_call x1, Pallas kernels, stage(): pl.pallas_call(stage_kernel, in_specs=[ANY], out_specs=VMEM, out_shape=pl...  3.4 us
  transfers between devices with their start and end apart: 3, of which 2 were waited for; matrix products, arithmetic and copies ran while one was open for 14% of the time, Pallas kernels for 3%

profile of v3, /device:TPU:0, one launch (start us, length us, event | category | flops | bytes accessed | tf_op | source)
XLA Modules:
  0.0 132.3 jit_solution(16187015070177047834)
XLA Ops:
  0.0 0.8 copy.9
  0.8 0.1 reshape.58.ids
  0.8 0.0 copy-start
  0.8 0.7 copy-done
  1.5 2.4 %pick.1 = bf16[8,64,4608]{2,1,0:T(8,128)(2,1)S(1)} custom-call(s32[32]{0:T(128)S(1)} %reshape.58.ids, s32[80]{0:T(128)S(1)} %copy-done, bf16[10,64,4096]{2,1,0:T(8,128)(2,1)} %down.1, bf16[10,64,512]{2,1,0:T(8,128)(2,1)} %up.1), custom_call_target="tpu_custom_call" | custom-call | tf_op jit(solution)/shard_map/pick/pallas_call | solution.py:55
  3.9 0.0 copy-start.4
  3.9 2.1 %copy-done.4 = bf16[8,64,4608]{2,1,0:T(8,128)(2,1)} copy-done((bf16[8,64,4608]{2,1,0:T(8,128)(2,1)}, bf16[8,64,4608]{2,1,0:T(8,128)(2,1)S(1)}, u32[]{:S(2)}) %copy-start.4) | copy-done | bytes 4718616
  6.0 7.5 %all-to-all-start = ((bf16[8,64,4608]{2,1,0:T(8,128)(2,1)}), bf16[8,64,4608]{2,1,0:T(8,128)(2,1)}, u32[]{:S(2)}, u32[]{:S(2)}) async-start(bf16[8,64,4608]{2,1,0:T(8,128)(2,1)} %copy-done.4), calls=%async_computation | async-start | bytes 9437184 | tf_op jit(solution)/shard_map/all_to_all | solution.py:225
  13.5 8.1 %fusion.2 = f32[1024,512]{1,0:T(8,128)S(1)} fusion(bf16[1024,4096]{1,0:T(8,128)(2,1)} %source, bf16[4096,1024]{1,0:T(8,128)(2,1)} %param.8, s32[]{:T(128)S(6)} %select_n.25), kind=kOutput, calls=%fused_computation.3 | convolution fusion | flops 4294967296 | bytes 14680068 | tf_op jit(solution)/shard_map/dot_general | solution.py:232
  21.7 0.1 collective-permute-start
  21.8 0.0 copy-start.5
  21.8 0.0 copy-start.6
  21.8 0.0 copy-start.1
  21.8 3.4 %stage.1.tokens = bf16[1024,4096]{1,0:T(8,128)(2,1)S(1)} custom-call(bf16[1024,4096]{1,0:T(8,128)(2,1)} %source), custom_call_target="tpu_custom_call" | custom-call | bytes 16777216 | tf_op jit(solution)/shard_map/stage/pallas_call | solution.py:80
  25.2 0.0 copy-start.2
  25.2 3.2 %copy-done.2 = bf16[1024,4096]{1,0:T(8,128)(2,1)} copy-done((bf16[1024,4096]{1,0:T(8,128)(2,1)}, bf16[1024,4096]{1,0:T(8,128)(2,1)S(1)}, u32[]{:S(2)}) %copy-start.2) | copy-done | bytes 8388632
  28.4 0.0 copy-done.5
  28.4 0.2 dynamic-slice_reduce_fusion
  28.6 0.0 copy-done.6
  28.6 0.2 reduce-window.9
  28.8 0.0 copy-done.1
  28.8 0.6 gather_fusion
  29.5 0.0 collective-permute-done
  29.5 9.7 %fusion.4.refs_2_ = f32[1024,512]{1,0:T(8,128)S(1)} fusion(f32[1024,512]{1,0:T(8,128)} %collective-permute-done, bf16[1024,4096]{1,0:T(8,128)(2,1)} %source, bf16[4096,1024]{1,0:T(8,128)(2,1)} %param.8, s32[]{:T(128)S(6)} %select_n.26), kind=kOutput, calls=%fused_computation.5 | convolution fusion | flops 4295491584 | bytes 16777220 | tf_op jit(solution)/shard_map/dot_general | solution.py:232
  39.2 78.8 %all-to-all-done.blocks.refs_3_.refs_4_.refs_5_.refs_6_ = bf16[8,64,4608]{2,1,0:T(8,128)(2,1)} async-done(((bf16[8,64,4608]{2,1,0:T(8,128)(2,1)}), bf16[8,64,4608]{2,1,0:T(8,128)(2,1)}, u32[]{:S(2)}, u32[]{:S(2)}) %all-to-all-start) | async-done | bytes 4718624 | tf_op jit(solution)/shard_map/all_to_all | solution.py:225
  118.0 0.0 copy-start.3
  118.0 3.4 %copy-done.3 = bf16[1024,4096]{1,0:T(8,128)(2,1)S(1)} copy-done((bf16[1024,4096]{1,0:T(8,128)(2,1)S(1)}, bf16[1024,4096]{1,0:T(8,128)(2,1)}, u32[]{:S(2)}) %copy-start.3) | copy-done | bytes 8388632
  121.4 4.7 %codes.1.refs_0_ = f32[512,128]{1,0:T(8,128)S(1)} custom-call(s32[4]{0:T(128)S(1)} %and_select_fusion.place, s32[4]{0:T(128)S(1)} %bitcast.8, bf16[1024,4096]{1,0:T(8,128)(2,1)S(1)} %copy-done.3, bf16[8,64,4608]{2,1,0:T(8,128)(2,1)} %all-to-all-done.blocks.refs_3_.refs_4_.refs_5_.refs_6_), custom_call_target="tpu_custom_call" | custom-call | flops 2147483648 | bytes 2097152 | tf_op jit(solution)/shard_map/codes/pallas_call | solution.py:129
  126.1 0.1 collective-permute-start.1
  126.2 1.5 %collective-permute-done.1.refs_1_ = f32[512,128]{1,0:T(8,128)S(1)} collective-permute-done((f32[512,128]{1,0:T(8,128)S(1)}, f32[512,128]{1,0:T(8,128)S(1)}, u32[]{:S(2)}, u32[]{:S(2)}) %collective-permute-start.1) | collective-permute-done | bytes 262176 | tf_op jit(solution)/shard_map/ppermute | solution.py:214
  127.8 4.5 %finish.1 = bf16[1024,512]{1,0:T(8,128)(2,1)} custom-call(s32[4]{0:T(128)S(1)} %and_select_fusion.place, s32[4]{0:T(128)S(1)} %bitcast.9, f32[512,128]{1,0:T(8,128)S(1)} %codes.1.refs_0_, f32[512,128]{1,0:T(8,128)S(1)} %collective-permute-done.1.refs_1_, f32[1024,512]{1,0:T(8,128)S(1)} %fusion.4.refs_2_, ...), custom_call_target="tpu_custom_call" | custom-call | tf_op jit(solution)/shard_map/finish/pallas_call | solution.py:188
  (3 shorter events, 0.0 us)
Async XLA Ops:
  0.8 0.7 copy-start
  3.9 2.1 %copy-start.4 = (bf16[8,64,4608]{2,1,0:T(8,128)(2,1)}, bf16[8,64,4608]{2,1,0:T(8,128)(2,1)S(1)}, u32[]{:S(2)}) copy-start(bf16[8,64,4608]{2,1,0:T(8,128)(2,1)S(1)} %pick.1) | copy-start | bytes 14155780
  6.0 112.0 %all-to-all-start = ((bf16[8,64,4608]{2,1,0:T(8,128)(2,1)}), bf16[8,64,4608]{2,1,0:T(8,128)(2,1)}, u32[]{:S(2)}, u32[]{:S(2)}) async-start(bf16[8,64,4608]{2,1,0:T(8,128)(2,1)} %copy-done.4), calls=%async_computation | async-start | bytes 9437184 | tf_op jit(solution)/shard_map/all_to_all | solution.py:225
  21.7 7.8 %collective-permute-start = (f32[1024,512]{1,0:T(8,128)S(1)}, f32[1024,512]{1,0:T(8,128)}, u32[]{:S(2)}, u32[]{:S(2)}) collective-permute-start(f32[1024,512]{1,0:T(8,128)S(1)} %fusion.2), channel_id=1, source_target_pairs={{0,1},{1,0},{2,3},{3,2},{4,5},{5,4},{6,7},{7,6},{8,9},{9,8},{10,11... | collective-permute-start | bytes 6291464 | tf_op jit(solution)/shard_map/ppermute | solution.py:234
  21.8 6.7 %copy-start.5 = (s32[8,4]{0,1:T(4,128)S(1)}, s32[8,4]{0,1:T(4,128)}, u32[]{:S(2)}) copy-start(s32[8,4]{0,1:T(4,128)} %param.11) | copy-start | bytes 388
  21.8 6.9 %copy-start.6 = (s32[1,4]{1,0:T(1,128)S(1)}, s32[1,4]{1,0:T(1,128)}, u32[]{:S(2)}) copy-start(s32[1,4]{1,0:T(1,128)} %param.12) | copy-start | bytes 52
  21.8 7.0 %copy-start.1 = (s32[80]{0:T(128)S(1)}, s32[80]{0:T(128)}, u32[]{:S(2)}) copy-start(s32[80]{0:T(128)} %owner_map.1) | copy-start | bytes 964
  25.2 3.2 %copy-start.2 = (bf16[1024,4096]{1,0:T(8,128)(2,1)}, bf16[1024,4096]{1,0:T(8,128)(2,1)S(1)}, u32[]{:S(2)}) copy-start(bf16[1024,4096]{1,0:T(8,128)(2,1)S(1)} %stage.1.tokens) | copy-start | bytes 25165828
  118.0 3.4 %copy-start.3 = (bf16[1024,4096]{1,0:T(8,128)(2,1)S(1)}, bf16[1024,4096]{1,0:T(8,128)(2,1)}, u32[]{:S(2)}) copy-start(bf16[1024,4096]{1,0:T(8,128)(2,1)} %copy-done.2) | copy-start | bytes 25165828
  126.1 1.6 %collective-permute-start.1 = (f32[512,128]{1,0:T(8,128)S(1)}, f32[512,128]{1,0:T(8,128)S(1)}, u32[]{:S(2)}, u32[]{:S(2)}) collective-permute-start(f32[512,128]{1,0:T(8,128)S(1)} %codes.1.refs_0_), channel_id=1, source_target_pairs={{0,1},{1,0},{2,3},{3,2},{4,5},{5,4},{6,7},{7,6},{8,9},{9,8},{10,11... | collective-permute-start | bytes 786440 | tf_op jit(solution)/shard_map/ppermute | solution.py:214

commit v4 on v0

v4 whole, which is shorter than its diff:
```python
import functools

import jax
import jax.numpy as jnp
from jax import lax
from jax.experimental import pallas as pl
from jax.experimental.pallas import tpu as pltpu
from jax.sharding import PartitionSpec as P

ADAPTER_SCALE = 2.0
MIB = 1 << 20
ANY = pl.BlockSpec(memory_space=pl.ANY)
VMEM = pl.BlockSpec(memory_space=pltpu.VMEM)


def in_hbm(x):
    return pltpu.with_memory_space_constraint(x, pltpu.HBM)


def pick_kernel(swaps, req, ids, owner_map, down, up, *refs):
    outs, (hold, wanted, in_sem, out_sem) = refs[: len(swaps)], refs[len(swaps) :]
    held, _, width = down.shape
    member = lax.axis_index("dp")
    for i, swap in enumerate(swaps):
        wanted[i] = 0
        for r in range(req):
            slot = owner_map[ids[r, member ^ swap]] - member * held

            @pl.when((slot >= 0) & (slot < held))
            def _(i=i, slot=slot):
                wanted[i] = 1
                to = hold.at[i]
                pltpu.make_async_copy(
                    down.at[slot], to.at[:, pl.ds(0, width)], in_sem.at[i]
                ).start()
                pltpu.make_async_copy(
                    up.at[slot], to.at[:, pl.ds(width, up.shape[2])], in_sem.at[i]
                ).start()

    for i, out in enumerate(outs):

        @pl.when(wanted[i] == 1)
        def _(i=i, out=out):
            pltpu.make_async_copy(hold.at[i], hold.at[i], in_sem.at[i]).wait()
            pltpu.make_async_copy(hold.at[i], out, out_sem.at[i]).start()

    for i, out in enumerate(outs):

        @pl.when(wanted[i] == 1)
        def _(i=i, out=out):
            pltpu.make_async_copy(hold.at[i], out, out_sem.at[i]).wait()


def pick(swaps, adapter_ids, owner_map, down_pool, up_pool):
    rows, req = adapter_ids.shape
    rank, width = down_pool.shape[1:]
    block = (rank, width + up_pool.shape[2])
    many = len(swaps)
    return pl.pallas_call(
        functools.partial(pick_kernel, swaps, req),
        grid_spec=pltpu.PrefetchScalarGridSpec(
            num_scalar_prefetch=2,
            grid=(),
            in_specs=[ANY, ANY],
            out_specs=[ANY] * many,
            scratch_shapes=[
                pltpu.VMEM((many, *block), down_pool.dtype),
                pltpu.SMEM((many,), jnp.int32),
                pltpu.SemaphoreType.DMA((many,)),
                pltpu.SemaphoreType.DMA((many,)),
            ],
        ),
        out_shape=[jax.ShapeDtypeStruct(block, down_pool.dtype)] * many,
        compiler_params=pltpu.CompilerParams(vmem_limit_bytes=48 * MIB),
        name="pick",
    )(adapter_ids.T, owner_map, in_hbm(down_pool), in_hbm(up_pool))


def dense_kernel(index, down, up, out):
    width = down.shape[2]
    out[:, :, :width] = down[...]
    out[:, :, width:] = up[...]


def dense(adapter_ids, owner_map, down_pool, up_pool):
    held, rank, width = down_pool.shape
    columns = up_pool.shape[2]
    slots = owner_map[adapter_ids] - lax.axis_index("dp") * held
    here = (slots >= 0) & (slots < held)
    index = jnp.sum(jnp.where(here, slots, 0), axis=1).astype(jnp.int32)
    many = index.shape[0]
    send = pl.pallas_call(
        dense_kernel,
        grid_spec=pltpu.PrefetchScalarGridSpec(
            num_scalar_prefetch=1,
            grid=(many,),
            in_specs=[
                pl.BlockSpec((1, rank, width), lambda j, index: (index[j], 0, 0)),
                pl.BlockSpec((1, rank, columns), lambda j, index: (index[j], 0, 0)),
            ],
            out_specs=pl.BlockSpec((1, rank, width + columns), lambda j, index: (j, 0, 0)),
        ),
        out_shape=jax.ShapeDtypeStruct((many, rank, width + columns), down_pool.dtype),
        name="pick_all",
    )(index, down_pool, up_pool)
    return lax.all_to_all(send, "dp", split_axis=0, concat_axis=0, tiled=True)


def request_of_rows(ends, count, first, rows):
    at = first + lax.broadcasted_iota(jnp.int32, (rows, 1), 0)
    which = jnp.zeros((rows, 1), jnp.int32)
    for r in range(count - 1):
        which += (at >= ends[r]).astype(jnp.int32)
    return which


def code_kernel(count, chunks, place, ends, tokens, *refs):
    n = len(refs) - 7
    blocks, (out, up, down, rows, total, block_sem, row_sem) = refs[:n], refs[n:]
    rank, features = out.shape[1] // 2, tokens.shape[1]
    columns = up.shape[1]
    step = features // chunks

    def parts(block):
        cuts = [(k * step, step) for k in range(chunks)]
        return [block.at[:, pl.ds(*cut)] for cut in cuts] + [block.at[:, pl.ds(features, columns)]]

    def targets(r):
        mine = pl.ds(r * rank, rank)
        return [down.at[k, mine, :] for k in range(chunks)] + [up.at[mine, :]]

    def load(r, block):
        for k, (source, target) in enumerate(zip(parts(block), targets(r))):
            pltpu.make_async_copy(source, target, block_sem.at[k]).start()

    for r in range(count):
        if n == 1:
            load(r, blocks[0].at[place[r]])
        else:
            for s, block in enumerate(blocks):

                @pl.when(place[r] == s)
                def _(r=r, block=block):
                    load(r, block)

    for k in range(chunks):
        pltpu.make_async_copy(
            tokens.at[:, pl.ds(k * step, step)], rows.at[k], row_sem.at[k]
        ).start()
    for k in range(chunks):
        pltpu.make_async_copy(down.at[k], down.at[k], block_sem.at[k]).wait()
        pltpu.make_async_copy(rows.at[k], rows.at[k], row_sem.at[k]).wait()
        part = lax.dot_general(
            rows[k], down[k], (((1,), (1,)), ((), ())), preferred_element_type=jnp.float32
        )
        if k == 0:
            total[...] = part
        elif k < chunks - 1:
            total[...] += part
        else:
            full = total[...] + part
    pltpu.make_async_copy(up, up, block_sem.at[chunks]).wait()
    which = request_of_rows(ends, count, 0, full.shape[0])
    code = full[:, :rank]
    for r in range(1, count):
        code = jnp.where(which == r, full[:, r * rank : (r + 1) * rank], code)
    half = full.shape[0] // 2
    out[...] = jnp.concatenate([code[:half], code[half:]], axis=1)


def codes(place, ends, tokens, blocks, columns):
    many, features = tokens.shape
    count = place.shape[0]
    rank = blocks[0].shape[-2]
    chunks = 4
    return pl.pallas_call(
        functools.partial(code_kernel, count, chunks),
        grid_spec=pltpu.PrefetchScalarGridSpec(
            num_scalar_prefetch=2,
            grid=(),
            in_specs=[ANY] * (1 + len(blocks)),
            out_specs=[VMEM, VMEM],
            scratch_shapes=[
                pltpu.VMEM((chunks, count * rank, features // chunks), tokens.dtype),
                pltpu.VMEM((chunks, many, features // chunks), tokens.dtype),
                pltpu.VMEM((many, count * rank), jnp.float32),
                pltpu.SemaphoreType.DMA((chunks + 1,)),
                pltpu.SemaphoreType.DMA((chunks,)),
            ],
        ),
        out_shape=[
            jax.ShapeDtypeStruct((many // 2, 2 * rank), jnp.float32),
            jax.ShapeDtypeStruct((count * rank, columns), tokens.dtype),
        ],
        compiler_params=pltpu.CompilerParams(vmem_limit_bytes=48 * MIB),
        name="codes",
    )(place, ends, in_hbm(tokens), *blocks)


def finish_kernel(count, parts, tile, ends, *refs):
    code_parts, (base, up, out, hold, sem) = refs[:parts], refs[parts:]
    rank = up.shape[0] // count
    code = code_parts[0][...]
    for p in range(1, parts):
        code = code + code_parts[p][...]
    half = code.shape[0]
    copies = []
    for i in range(out.shape[0] // tile):
        first = i * tile
        side, at = first // half, first % half
        mine = code[at : at + tile, side * rank : (side + 1) * rank]
        which = request_of_rows(ends, count, first, tile)
        zero = jnp.zeros_like(mine)
        wide = jnp.concatenate([jnp.where(which == r, mine, zero) for r in range(count)], axis=1)
        delta = None
        for _ in range(3):
            part = wide.astype(jnp.bfloat16)
            wide = wide - part.astype(jnp.float32)
            term = jnp.dot(part, up[...], preferred_element_type=jnp.float32)
            delta = term if delta is None else delta + term
        rows = pl.ds(first, tile)
        hold[rows, :] = (base[rows, :] + ADAPTER_SCALE * delta).astype(hold.dtype)
        copies.append(pltpu.make_async_copy(hold.at[rows, :], out.at[rows, :], sem.at[i]))
        copies[-1].start()
    for copy in copies:
        copy.wait()


def finish(ends, code_parts, base, up):
    many, columns = base.shape
    count = ends.shape[0]
    parts = len(code_parts)
    tile = min(256, many // 2)
    return pl.pallas_call(
        functools.partial(finish_kernel, count, parts, tile),
        grid_spec=pltpu.PrefetchScalarGridSpec(
            num_scalar_prefetch=1,
            grid=(),
            in_specs=[VMEM] * (parts + 2),
            out_specs=ANY,
            scratch_shapes=[
                pltpu.VMEM((many, columns), jnp.bfloat16),
                pltpu.SemaphoreType.DMA((many // tile,)),
            ],
        ),
        out_shape=jax.ShapeDtypeStruct((many, columns), jnp.bfloat16),
        compiler_params=pltpu.CompilerParams(vmem_limit_bytes=24 * MIB),
        name="finish",
    )(ends, *code_parts, pltpu.with_memory_space_constraint(base, pltpu.VMEM), up)


def gathered(part, axis, size):
    held = [part]
    for step in range(1, size):
        held.append(lax.ppermute(part, axis, [(i, (i + step) % size) for i in range(size)]))
    return held


def shards(sizes, tokens, key_weight, down_pool, up_pool, adapter_ids, lengths, owner_map):
    n_groups, n_dp, n_tensor = sizes
    held, _, width = down_pool.shape
    columns = up_pool.shape[2]

    member = lax.axis_index("dp")
    if n_dp == 8:
        swaps = [4, 5, 6, 7, 2, 3, 1]
        sends = pick(swaps, adapter_ids, owner_map, down_pool, up_pool)
        *sends, late_tokens = lax.optimization_barrier((*sends, tokens))
        got = {}
        for swap, send in zip(swaps, sends):
            got[swap] = lax.ppermute(send, "dp", [(i, i ^ swap) for i in range(n_dp)])
        blocks = [got[swap] for swap in range(1, n_dp)]
    else:
        late_tokens = tokens
        blocks = [dense(adapter_ids, owner_map, down_pool, up_pool)]

    me = lax.axis_index("tensor")
    base = None
    for step in reversed(range(n_tensor)):
        to = lax.rem(me + step, n_tensor)
        weight = lax.dynamic_slice_in_dim(key_weight, to * columns, columns, 1)
        part = jnp.dot(late_tokens, weight, preferred_element_type=jnp.float32)
        if step:
            part = lax.ppermute(
                part, "tensor", [(i, (i + step) % n_tensor) for i in range(n_tensor)]
            )
        base = part if base is None else base + part
    my_ids = lax.dynamic_index_in_dim(adapter_ids, member, 0, keepdims=False)
    my_slots = owner_map[my_ids]
    place = my_slots // held
    ends = jnp.cumsum(lengths[0]).astype(jnp.int32)
    if n_dp == 8:
        place = place ^ member
        own = jnp.clip(jnp.max(jnp.where(place == 0, my_slots % held, 0)), 0, held - 1)
        own_down = lax.dynamic_index_in_dim(down_pool, own, 0, keepdims=False)
        own_up = lax.dynamic_index_in_dim(up_pool, own, 0, keepdims=False)
        blocks = [jnp.concatenate([own_down, own_up], axis=1)] + blocks

    *blocks, base, place, ends = lax.optimization_barrier((*blocks, base, place, ends))
    code, up = codes(place, ends, tokens, blocks, columns)
    code_parts = gathered(code, "tensor", n_tensor)
    return finish(ends, code_parts, base, up)


def solution(mesh):
    placed = (
        P(("groups", "dp"), "tensor"),
        P("tensor", None),
        P("dp", None, "tensor"),
        P("dp", None, "tensor"),
        P("groups", None),
        P(("groups", "dp"), None),
        P("groups"),
    )
    sizes = tuple(mesh.shape[name] for name in ("groups", "dp", "tensor"))
    return jax.shard_map(
        functools.partial(shards, sizes),
        mesh=mesh,
        in_specs=placed,
        out_specs=P(("groups", "dp"), "tensor"),
        check_vma=False,
    )
```

time: 216 us -> 138 us (0.64)
  the two profiles are of different devices: /device:TPU:0 before, /device:TPU:9 now
where the time goes in v4:
time: 138 us; the launch traced here: 137 us
  waiting for transfers between devices  81.4 us (59%)
  matrix products  20.4 us (15%)
  starting transfers between devices  13.9 us (10%)
  Pallas kernels  12.5 us (9%)
  local copies, waits for them, and re-layouts  6.35 us (5%)
  other arithmetic  2.04 us (1%)
    ppermute x7, waiting for transfers between devices, shards(): got[swap] = lax.ppermute(send, 'dp', [(i, i ^ swap) for i in range(n_dp)])  80.2 us
    dot_general x2, matrix products, shards(): part = jnp.dot(late_tokens, weight, preferred_element_type=jnp.float32)  20.4 us
    ppermute x7, starting transfers between devices, shards(): got[swap] = lax.ppermute(send, 'dp', [(i, i ^ swap) for i in range(n_dp)])  11.7 us
    pallas_call x1, Pallas kernels, codes(): pl.pallas_call(functools.partial(code_kernel, count, chunks), grid_spec=p...  8.23 us
  transfers between devices with their start and end apart: 9, of which 7 were waited for; matrix products, arithmetic and copies ran while one was open for 12% of the time, Pallas kernels for 0%

profile of v4, /device:TPU:9, one launch (start us, length us, event | category | flops | bytes accessed | tf_op | source)
XLA Modules:
  0.0 137.3 jit_solution(1338979203520788559)
XLA Ops:
  0.0 0.7 copy-done
  0.7 0.7 copy-done.2
  1.3 2.0 %pick.1 = (bf16[64,4608]{1,0:T(8,128)(2,1)S(1)}, bf16[64,4608]{1,0:T(8,128)(2,1)S(1)}, bf16[64,4608]{1,0:T(8,128)(2,1)S(1)}, bf16[64,4608]{1,0:T(8,128)(2,1)S(1)...) custom-call(s32[4,8]{1,0:T(4,128)S(1)} %bitcast.13, s32[80]{0:T(128)S(1)} %copy-done, ...), custom_call_target="tpu_custom_call" | custom-call | tf_op jit(solution)/shard_map/pick/pallas_call | solution.py:59
  3.3 0.8 copy-done.4
  4.2 10.6 %fusion.2 = f32[1024,512]{1,0:T(8,128)} fusion(bf16[1024,4096]{1,0:T(8,128)(2,1)} %tokens.1, bf16[4096,1024]{1,0:T(8,128)(2,1)} %param.8, s32[]{:T(128)S(6)} %select_n.45), kind=kOutput, calls=%fused_computation.3 | convolution fusion | flops 4294967296 | bytes 14680068 | tf_op jit(solution)/shard_map/dot_general | solution.py:282
  14.8 0.7 collective-permute-start.7
  15.5 2.2 %collective-permute-start = (bf16[64,4608]{1,0:T(8,128)(2,1)}, bf16[64,4608]{1,0:T(8,128)(2,1)S(1)}, u32[]{:S(2)}, u32[]{:S(2)}) collective-permute-start(bf16[64,4608]{1,0:T(8,128)(2,1)} %get-tuple-element.40), channel_id=1, source_target_pairs={{0,2},{2,0},{4,6},{6,4},{8,10},{10,8},{12,14},{14,12},{1,3},{3,1},... | collective-permute-start | bytes 1769480 | tf_op jit(solution)/shard_map/ppermute | solution.py:271
  17.7 0.3 collective-permute-start.1
  18.0 0.8 collective-permute-start.2
  18.9 3.3 %collective-permute-start.3 = (bf16[64,4608]{1,0:T(8,128)(2,1)}, bf16[64,4608]{1,0:T(8,128)(2,1)S(1)}, u32[]{:S(2)}, u32[]{:S(2)}) collective-permute-start(bf16[64,4608]{1,0:T(8,128)(2,1)} %copy-done.5), channel_id=1, source_target_pairs={{0,8},{2,10},{4,12},{6,14},{8,0},{10,2},{12,4},{14,6},{1,9},{3,11}... | collective-permute-start | bytes 1769480 | tf_op jit(solution)/shard_map/ppermute | solution.py:271
  22.2 0.2 dynamic-slice_reduce_fusion
  22.4 0.6 gather_fusion
  23.0 0.7 fusion.11
  24.5 1.9 %dynamic-slice_bitcast_fusion = bf16[64,4096]{1,0:T(8,128)(2,1)} fusion(bf16[10,64,4096]{2,1,0:T(8,128)(2,1)} %down.1, s32[]{:T(128)S(6)} %min.4), kind=kLoop, calls=%fused_computation.7 | loop fusion | bytes 1048580 | tf_op jit(solution)/shard_map/jit(dynamic_index_in_dim)/squeeze | solution.py:295
  26.3 1.5 %dynamic-slice_bitcast_fusion.1 = bf16[64,512]{1,0:T(8,128)(2,1)} fusion(bf16[10,64,512]{2,1,0:T(8,128)(2,1)} %up.1, s32[]{:T(128)S(6)} %min.4), kind=kLoop, calls=%fused_computation.8 | loop fusion | bytes 131076 | tf_op jit(solution)/shard_map/jit(dynamic_index_in_dim)/squeeze | solution.py:296
  27.8 0.2 reduce-window.9
  28.0 1.1 pad_maximum_fusion.refs_0_
  29.1 2.5 %collective-permute-done.refs_1_ = bf16[64,4608]{1,0:T(8,128)(2,1)S(1)} collective-permute-done((bf16[64,4608]{1,0:T(8,128)(2,1)}, bf16[64,4608]{1,0:T(8,128)(2,1)S(1)}, u32[]{:S(2)}, u32[]{:S(2)}) %collective-permute-start) | collective-permute-done | bytes 589856 | tf_op jit(solution)/shard_map/ppermute | solution.py:271
  31.6 4.3 %collective-permute-start.4 = (bf16[64,4608]{1,0:T(8,128)(2,1)}, bf16[64,4608]{1,0:T(8,128)(2,1)S(1)}, u32[]{:S(2)}, u32[]{:S(2)}) collective-permute-start(bf16[64,4608]{1,0:T(8,128)(2,1)} %copy-done.4), channel_id=1, source_target_pairs={{0,10},{2,8},{4,14},{6,12},{8,2},{10,0},{12,6},{14,4},{1,11},{3,9}... | collective-permute-start | bytes 1769480 | tf_op jit(solution)/shard_map/ppermute | solution.py:271
  35.9 19.8 %collective-permute-done.1.refs_2_ = bf16[64,4608]{1,0:T(8,128)(2,1)S(1)} collective-permute-done((bf16[64,4608]{1,0:T(8,128)(2,1)}, bf16[64,4608]{1,0:T(8,128)(2,1)S(1)}, u32[]{:S(2)}, u32[]{:S(2)}) %collective-permute-start.1) | collective-permute-done | bytes 589856 | tf_op jit(solution)/shard_map/ppermute | solution.py:271
  55.7 0.0 collective-permute-start.5
  55.7 0.0 collective-permute-done.7
  55.7 0.7 collective-permute-start.6
  56.5 9.7 %fusion.4.refs_2_ = f32[1024,512]{1,0:T(8,128)S(1)} fusion(f32[1024,512]{1,0:T(8,128)} %collective-permute-done.7, bf16[1024,4096]{1,0:T(8,128)(2,1)} %tokens.1, bf16[4096,1024]{1,0:T(8,128)(2,1)} %param.8, s32[]{:T(128)S(6)} %select_n.46), kind=kOutput, calls=%fused_computation.5 | convolution fusion | flops 4295491584 | bytes 16777220 | tf_op jit(solution)/shard_map/dot_general | solution.py:282
  66.2 2.2 %collective-permute-done.2.refs_3_ = bf16[64,4608]{1,0:T(8,128)(2,1)S(1)} collective-permute-done((bf16[64,4608]{1,0:T(8,128)(2,1)}, bf16[64,4608]{1,0:T(8,128)(2,1)S(1)}, u32[]{:S(2)}, u32[]{:S(2)}) %collective-permute-start.2) | collective-permute-done | bytes 589856 | tf_op jit(solution)/shard_map/ppermute | solution.py:271
  68.4 30.4 %collective-permute-done.4.refs_5_ = bf16[64,4608]{1,0:T(8,128)(2,1)S(1)} collective-permute-done((bf16[64,4608]{1,0:T(8,128)(2,1)}, bf16[64,4608]{1,0:T(8,128)(2,1)S(1)}, u32[]{:S(2)}, u32[]{:S(2)}) %collective-permute-start.4) | collective-permute-done | bytes 589856 | tf_op jit(solution)/shard_map/ppermute | solution.py:271
  98.7 12.5 %collective-permute-done.5.refs_6_ = bf16[64,4608]{1,0:T(8,128)(2,1)S(1)} collective-permute-done((bf16[64,4608]{1,0:T(8,128)(2,1)S(1)}, bf16[64,4608]{1,0:T(8,128)(2,1)S(1)}, u32[]{:S(2)}, u32[]{:S(2)}) %collective-permute-start.5) | collective-permute-done | bytes 589856 | tf_op jit(solution)/shard_map/ppermute | solution.py:271
  111.3 12.8 %collective-permute-done.6.refs_7_ = bf16[64,4608]{1,0:T(8,128)(2,1)S(1)} collective-permute-done((bf16[64,4608]{1,0:T(8,128)(2,1)S(1)}, bf16[64,4608]{1,0:T(8,128)(2,1)S(1)}, u32[]{:S(2)}, u32[]{:S(2)}) %collective-permute-start.6) | collective-permute-done | bytes 589856 | tf_op jit(solution)/shard_map/ppermute | solution.py:271
  124.1 8.2 %codes.1 = (f32[512,128]{1,0:T(8,128)S(1)}, bf16[256,512]{1,0:T(8,128)(2,1)S(1)}) custom-call(s32[4]{0:T(128)S(1)} %get-tuple-element.49.place, s32[4]{0:T(128)S(1)} %bitcast.14, bf16[1024,4096]{1,0:T(8,128)(2,1)} %tokens.1, bf16[64,4608]{1,0:T(8,128)(2,1)S(1)} %pad_maximum_fusion.refs_0_, bf16[64,4608]{1,0:T(8,128)(2,1)S(1)} %collective-permute-done.refs_1_, ...), custom_call_target="tpu_custom_call" | custom-call | tf_op jit(solution)/shard_map/codes/pallas_call | solution.py:176
  132.3 1.5 %collective-permute-start.8 = (f32[512,128]{1,0:T(8,128)S(1)}, f32[512,128]{1,0:T(8,128)S(1)}, u32[]{:S(2)}, u32[]{:S(2)}) collective-permute-start(f32[512,128]{1,0:T(8,128)S(1)} %get-tuple-element.58.refs_0_), channel_id=1, source_target_pairs={{0,1},{1,0},{2,3},{3,2},{4,5},{5,4},{6,7},{7,6},{8,9},{9,8},{10,11... | collective-permute-start | bytes 786440 | tf_op jit(solution)/shard_map/ppermute | solution.py:255
  133.8 1.2 collective-permute-done.8.refs_1_
  135.0 2.3 %finish.1 = bf16[1024,512]{1,0:T(8,128)(2,1)} custom-call(s32[4]{0:T(128)S(1)} %bitcast.15, f32[512,128]{1,0:T(8,128)S(1)} %get-tuple-element.58.refs_0_, f32[512,128]{1,0:T(8,128)S(1)} %collective-permute-done.8.refs_1_, f32[1024,512]{1,0:T(8,128)S(1)} %fusion.4.refs_2_, bf16[256,512]{1,0:T(8,128)(2,1)S(1)} %get-tuple-element.60.refs_3_), custom_call_target="tpu_custom_call" | custom-call | tf_op jit(solution)/shard_map/finish/pallas_call | solution.py:234
  (14 shorter events, 0.0 us)
Async XLA Ops:
  0.0 0.7 copy-start
  0.7 0.7 copy-start.2
  3.3 0.8 copy-start.4
  4.1 10.6 %copy-start.5 = (bf16[64,4608]{1,0:T(8,128)(2,1)}, bf16[64,4608]{1,0:T(8,128)(2,1)S(1)}, u32[]{:S(2)}) copy-start(bf16[64,4608]{1,0:T(8,128)(2,1)S(1)} %get-tuple-element.43) | copy-start | bytes 1769476
  4.1 18.0 %copy-start.3 = (s32[8,4]{0,1:T(4,128)S(1)}, s32[8,4]{0,1:T(4,128)}, u32[]{:S(2)}) copy-start(s32[8,4]{0,1:T(4,128)} %param.11) | copy-start | bytes 388
  4.1 18.2 %copy-start.1 = (s32[80]{0:T(128)S(1)}, s32[80]{0:T(128)}, u32[]{:S(2)}) copy-start(s32[80]{0:T(128)} %owner_map.1) | copy-start | bytes 964
  4.1 23.7 %copy-start.6 = (s32[1,4]{1,0:T(1,128)S(1)}, s32[1,4]{1,0:T(1,128)}, u32[]{:S(2)}) copy-start(s32[1,4]{1,0:T(1,128)} %param.12) | copy-start | bytes 52
  14.8 40.9 %collective-permute-start.7 = (f32[1024,512]{1,0:T(8,128)}, f32[1024,512]{1,0:T(8,128)}, u32[]{:S(2)}, u32[]{:S(2)}) collective-permute-start(f32[1024,512]{1,0:T(8,128)} %fusion.2), channel_id=1, source_target_pairs={{0,1},{1,0},{2,3},{3,2},{4,5},{5,4},{6,7},{7,6},{8,9},{9,8},{10,11... | collective-permute-start | bytes 6291464 | tf_op jit(solution)/shard_map/ppermute | solution.py:284
  15.5 16.1 %collective-permute-start = (bf16[64,4608]{1,0:T(8,128)(2,1)}, bf16[64,4608]{1,0:T(8,128)(2,1)S(1)}, u32[]{:S(2)}, u32[]{:S(2)}) collective-permute-start(bf16[64,4608]{1,0:T(8,128)(2,1)} %get-tuple-element.40), channel_id=1, source_target_pairs={{0,2},{2,0},{4,6},{6,4},{8,10},{10,8},{12,14},{14,12},{1,3},{3,1},... | collective-permute-start | bytes 1769480 | tf_op jit(solution)/shard_map/ppermute | solution.py:271
  17.7 38.0 %collective-permute-start.1 = (bf16[64,4608]{1,0:T(8,128)(2,1)}, bf16[64,4608]{1,0:T(8,128)(2,1)S(1)}, u32[]{:S(2)}, u32[]{:S(2)}) collective-permute-start(bf16[64,4608]{1,0:T(8,128)(2,1)} %get-tuple-element.41), channel_id=1, source_target_pairs={{0,4},{2,6},{4,0},{6,2},{8,12},{10,14},{12,8},{14,10},{1,5},{3,7},... | collective-permute-start | bytes 1769480 | tf_op jit(solution)/shard_map/ppermute | solution.py:271
  18.0 50.3 %collective-permute-start.2 = (bf16[64,4608]{1,0:T(8,128)(2,1)}, bf16[64,4608]{1,0:T(8,128)(2,1)S(1)}, u32[]{:S(2)}, u32[]{:S(2)}) collective-permute-start(bf16[64,4608]{1,0:T(8,128)(2,1)} %get-tuple-element.42), channel_id=1, source_target_pairs={{0,6},{2,4},{4,2},{6,0},{8,14},{10,12},{12,10},{14,8},{1,7},{3,5},... | collective-permute-start | bytes 1769480 | tf_op jit(solution)/shard_map/ppermute | solution.py:271
  18.9 49.5 %collective-permute-start.3 = (bf16[64,4608]{1,0:T(8,128)(2,1)}, bf16[64,4608]{1,0:T(8,128)(2,1)S(1)}, u32[]{:S(2)}, u32[]{:S(2)}) collective-permute-start(bf16[64,4608]{1,0:T(8,128)(2,1)} %copy-done.5), channel_id=1, source_target_pairs={{0,8},{2,10},{4,12},{6,14},{8,0},{10,2},{12,4},{14,6},{1,9},{3,11}... | collective-permute-start | bytes 1769480 | tf_op jit(solution)/shard_map/ppermute | solution.py:271
  31.6 67.1 %collective-permute-start.4 = (bf16[64,4608]{1,0:T(8,128)(2,1)}, bf16[64,4608]{1,0:T(8,128)(2,1)S(1)}, u32[]{:S(2)}, u32[]{:S(2)}) collective-permute-start(bf16[64,4608]{1,0:T(8,128)(2,1)} %copy-done.4), channel_id=1, source_target_pairs={{0,10},{2,8},{4,14},{6,12},{8,2},{10,0},{12,6},{14,4},{1,11},{3,9}... | collective-permute-start | bytes 1769480 | tf_op jit(solution)/shard_map/ppermute | solution.py:271
  55.7 55.5 %collective-permute-start.5 = (bf16[64,4608]{1,0:T(8,128)(2,1)S(1)}, bf16[64,4608]{1,0:T(8,128)(2,1)S(1)}, u32[]{:S(2)}, u32[]{:S(2)}) collective-permute-start(bf16[64,4608]{1,0:T(8,128)(2,1)S(1)} %get-tuple-element.45), channel_id=1, source_target_pairs={{0,12},{2,14},{4,8},{6,10},{8,4},{10,6},{12,0},{14,2},{1,13},{3,15... | collective-permute-start | bytes 1769480 | tf_op jit(solution)/shard_map/ppermute | solution.py:271
  55.7 68.4 %collective-permute-start.6 = (bf16[64,4608]{1,0:T(8,128)(2,1)S(1)}, bf16[64,4608]{1,0:T(8,128)(2,1)S(1)}, u32[]{:S(2)}, u32[]{:S(2)}) collective-permute-start(bf16[64,4608]{1,0:T(8,128)(2,1)S(1)} %get-tuple-element.46), channel_id=1, source_target_pairs={{0,14},{2,12},{4,10},{6,8},{8,6},{10,4},{12,2},{14,0},{1,15},{3,13... | collective-permute-start | bytes 1769480 | tf_op jit(solution)/shard_map/ppermute | solution.py:271
  132.3 2.7 %collective-permute-start.8 = (f32[512,128]{1,0:T(8,128)S(1)}, f32[512,128]{1,0:T(8,128)S(1)}, u32[]{:S(2)}, u32[]{:S(2)}) collective-permute-start(f32[512,128]{1,0:T(8,128)S(1)} %get-tuple-element.58.refs_0_), channel_id=1, source_target_pairs={{0,1},{1,0},{2,3},{3,2},{4,5},{5,4},{6,7},{7,6},{8,9},{9,8},{10,11... | collective-permute-start | bytes 786440 | tf_op jit(solution)/shard_map/ppermute | solution.py:255

commit v5 on v4

v5 whole, which is shorter than its diff:
```python
import functools

import jax
import jax.numpy as jnp
from jax import lax
from jax.experimental import pallas as pl
from jax.experimental.pallas import tpu as pltpu
from jax.sharding import PartitionSpec as P

ADAPTER_SCALE = 2.0
MIB = 1 << 20
ANY = pl.BlockSpec(memory_space=pl.ANY)
VMEM = pl.BlockSpec(memory_space=pltpu.VMEM)


def in_hbm(x):
    return pltpu.with_memory_space_constraint(x, pltpu.HBM)


def pick_kernel(pieces, req, ids, owner_map, down, up, *refs):
    n = len(pieces)
    outs, holds = refs[:n], refs[n : 2 * n]
    wanted, in_sem, out_sem = refs[2 * n :]
    held = down.shape[0]
    member = lax.axis_index("dp")
    for i, (swap, lo, hi, with_up) in enumerate(pieces):
        wanted[i] = 0
        for r in range(req):
            slot = owner_map[ids[r, member ^ swap]] - member * held

            @pl.when((slot >= 0) & (slot < held))
            def _(i=i, slot=slot, lo=lo, hi=hi, with_up=with_up):
                wanted[i] = 1
                pltpu.make_async_copy(
                    down.at[slot, :, pl.ds(lo, hi - lo)],
                    holds[i].at[:, pl.ds(0, hi - lo)],
                    in_sem.at[i],
                ).start()
                if with_up:
                    pltpu.make_async_copy(
                        up.at[slot], holds[i].at[:, pl.ds(hi - lo, up.shape[2])], in_sem.at[i]
                    ).start()

    for i in range(n):

        @pl.when(wanted[i] == 1)
        def _(i=i):
            pltpu.make_async_copy(holds[i], holds[i], in_sem.at[i]).wait()
            pltpu.make_async_copy(holds[i], outs[i], out_sem.at[i]).start()

    for i in range(n):

        @pl.when(wanted[i] == 1)
        def _(i=i):
            pltpu.make_async_copy(holds[i], outs[i], out_sem.at[i]).wait()


def pick(pieces, adapter_ids, owner_map, down_pool, up_pool):
    rows, req = adapter_ids.shape
    rank = down_pool.shape[1]
    shapes = [(rank, hi - lo + up_pool.shape[2] * with_up) for _, lo, hi, with_up in pieces]
    many = len(pieces)
    return pl.pallas_call(
        functools.partial(pick_kernel, pieces, req),
        grid_spec=pltpu.PrefetchScalarGridSpec(
            num_scalar_prefetch=2,
            grid=(),
            in_specs=[ANY, ANY],
            out_specs=[ANY] * many,
            scratch_shapes=[pltpu.VMEM(shape, down_pool.dtype) for shape in shapes]
            + [
                pltpu.SMEM((many,), jnp.int32),
                pltpu.SemaphoreType.DMA((many,)),
                pltpu.SemaphoreType.DMA((many,)),
            ],
        ),
        out_shape=[jax.ShapeDtypeStruct(shape, down_pool.dtype) for shape in shapes],
        compiler_params=pltpu.CompilerParams(vmem_limit_bytes=48 * MIB),
        name="pick",
    )(adapter_ids.T, owner_map, in_hbm(down_pool), in_hbm(up_pool))


def dense_kernel(index, down, up, out):
    width = down.shape[2]
    out[:, :, :width] = down[...]
    out[:, :, width:] = up[...]


def dense(adapter_ids, owner_map, down_pool, up_pool):
    held, rank, width = down_pool.shape
    columns = up_pool.shape[2]
    slots = owner_map[adapter_ids] - lax.axis_index("dp") * held
    here = (slots >= 0) & (slots < held)
    index = jnp.sum(jnp.where(here, slots, 0), axis=1).astype(jnp.int32)
    many = index.shape[0]
    send = pl.pallas_call(
        dense_kernel,
        grid_spec=pltpu.PrefetchScalarGridSpec(
            num_scalar_prefetch=1,
            grid=(many,),
            in_specs=[
                pl.BlockSpec((1, rank, width), lambda j, index: (index[j], 0, 0)),
                pl.BlockSpec((1, rank, columns), lambda j, index: (index[j], 0, 0)),
            ],
            out_specs=pl.BlockSpec((1, rank, width + columns), lambda j, index: (j, 0, 0)),
        ),
        out_shape=jax.ShapeDtypeStruct((many, rank, width + columns), down_pool.dtype),
        name="pick_all",
    )(index, down_pool, up_pool)
    return lax.all_to_all(send, "dp", split_axis=0, concat_axis=0, tiled=True)


def request_of_rows(ends, count, first, rows):
    at = first + lax.broadcasted_iota(jnp.int32, (rows, 1), 0)
    which = jnp.zeros((rows, 1), jnp.int32)
    for r in range(count - 1):
        which += (at >= ends[r]).astype(jnp.int32)
    return which


def code_kernel(count, cut, step, kinds, has_up, has_before, index, ends, tokens, *refs):
    lo, hi = cut
    chunks = (hi - lo) // step
    n = sum(2 if kind == "pool" else 1 for kind, _, _ in kinds)
    arrays, refs = list(refs[:n]), list(refs[n:])
    before = refs.pop(0) if has_before else None
    out = refs.pop(0)
    up = refs.pop(0) if has_up else None
    down, rows, total, block_sem, row_sem = refs
    rank = out.shape[1] // 2

    def load(r, down_block, first, up_block):
        mine = pl.ds(r * rank, rank)
        for k in range(chunks):
            pltpu.make_async_copy(
                down_block.at[:, pl.ds(first + k * step, step)],
                down.at[k, mine, :],
                block_sem.at[k],
            ).start()
        if has_up:
            pltpu.make_async_copy(up_block, up.at[mine, :], block_sem.at[chunks]).start()

    def load_from(r, kind, first, up_first, held):
        block = held[0]
        if kind != "plain":
            block = block.at[index[count + r]]
        up_block = None
        if has_up:
            width = up.shape[1]
            if kind == "pool":
                up_block = held[1].at[index[count + r]]
            else:
                up_block = block.at[:, pl.ds(up_first, width)]
        load(r, block, first, up_block)

    for r in range(count):
        at = 0
        for s, (kind, first, up_first) in enumerate(kinds):
            width = 2 if kind == "pool" else 1
            held, at = arrays[at : at + width], at + width
            if len(kinds) == 1:
                load_from(r, kind, first, up_first, held)
            else:

                @pl.when(index[r] == s)
                def _(r=r, kind=kind, first=first, up_first=up_first, held=held):
                    load_from(r, kind, first, up_first, held)

    for k in range(chunks):
        pltpu.make_async_copy(
            tokens.at[:, pl.ds(lo + k * step, step)], rows.at[k], row_sem.at[k]
        ).start()
    for k in range(chunks):
        pltpu.make_async_copy(down.at[k], down.at[k], block_sem.at[k]).wait()
        pltpu.make_async_copy(rows.at[k], rows.at[k], row_sem.at[k]).wait()
        full = lax.dot_general(
            rows[k], down[k], (((1,), (1,)), ((), ())), preferred_element_type=jnp.float32
        )
        if k:
            full = total[...] + full
        if k < chunks - 1:
            total[...] = full
    if has_up:
        pltpu.make_async_copy(up, up, block_sem.at[chunks]).wait()
    which = request_of_rows(ends, count, 0, full.shape[0])
    code = full[:, :rank]
    for r in range(1, count):
        code = jnp.where(which == r, full[:, r * rank : (r + 1) * rank], code)
    half = full.shape[0] // 2
    code = jnp.concatenate([code[:half], code[half:]], axis=1)
    out[...] = code + before[...] if has_before else code


def codes(index, ends, tokens, sources, cut, step, columns=0, before=None):
    many = tokens.shape[0]
    count = ends.shape[0]
    rank = sources[0][1][0].shape[-2]
    chunks = (cut[1] - cut[0]) // step
    kinds = [(kind, first, up_first) for kind, _, first, up_first in sources]
    arrays = [array for _, held, _, _ in sources for array in held]
    out_shape = [jax.ShapeDtypeStruct((many // 2, 2 * rank), jnp.float32)]
    if columns:
        out_shape.append(jax.ShapeDtypeStruct((count * rank, columns), tokens.dtype))
    extra = [] if before is None else [before]
    return pl.pallas_call(
        functools.partial(
            code_kernel, count, cut, step, kinds, columns > 0, before is not None
        ),
        grid_spec=pltpu.PrefetchScalarGridSpec(
            num_scalar_prefetch=2,
            grid=(),
            in_specs=[ANY] * (1 + len(arrays)) + [VMEM] * len(extra),
            out_specs=[VMEM] * len(out_shape),
            scratch_shapes=[
                pltpu.VMEM((chunks, count * rank, step), tokens.dtype),
                pltpu.VMEM((chunks, many, step), tokens.dtype),
                pltpu.VMEM((many, count * rank), jnp.float32),
                pltpu.SemaphoreType.DMA((chunks + 1,)),
                pltpu.SemaphoreType.DMA((chunks,)),
            ],
        ),
        out_shape=out_shape,
        compiler_params=pltpu.CompilerParams(vmem_limit_bytes=40 * MIB),
        cost_estimate=pl.CostEstimate(
            flops=2 * many * (cut[1] - cut[0]) * count * rank,
            bytes_accessed=(cut[1] - cut[0]) * (many + count * rank) * 2,
            transcendentals=0,
        ),
        name="codes",
    )(index, ends, in_hbm(tokens), *arrays, *extra)


def finish_kernel(count, parts, tile, ends, *refs):
    code_parts, (base, up, out, hold, sem) = refs[:parts], refs[parts:]
    rank = up.shape[0] // count
    code = code_parts[0][...]
    for p in range(1, parts):
        code = code + code_parts[p][...]
    half = code.shape[0]
    copies = []
    for i in range(out.shape[0] // tile):
        first = i * tile
        side, at = first // half, first % half
        mine = code[at : at + tile, side * rank : (side + 1) * rank]
        which = request_of_rows(ends, count, first, tile)
        zero = jnp.zeros_like(mine)
        wide = jnp.concatenate([jnp.where(which == r, mine, zero) for r in range(count)], axis=1)
        delta = None
        for _ in range(3):
            part = wide.astype(jnp.bfloat16)
            wide = wide - part.astype(jnp.float32)
            term = jnp.dot(part, up[...], preferred_element_type=jnp.float32)
            delta = term if delta is None else delta + term
        rows = pl.ds(first, tile)
        hold[rows, :] = (base[rows, :] + ADAPTER_SCALE * delta).astype(hold.dtype)
        copies.append(pltpu.make_async_copy(hold.at[rows, :], out.at[rows, :], sem.at[i]))
        copies[-1].start()
    for copy in copies:
        copy.wait()


def finish(ends, code_parts, base, up):
    many, columns = base.shape
    count = ends.shape[0]
    parts = len(code_parts)
    tile = min(256, many // 2)
    return pl.pallas_call(
        functools.partial(finish_kernel, count, parts, tile),
        grid_spec=pltpu.PrefetchScalarGridSpec(
            num_scalar_prefetch=1,
            grid=(),
            in_specs=[VMEM] * (parts + 2),
            out_specs=ANY,
            scratch_shapes=[
                pltpu.VMEM((many, columns), jnp.bfloat16),
                pltpu.SemaphoreType.DMA((many // tile,)),
            ],
        ),
        out_shape=jax.ShapeDtypeStruct((many, columns), jnp.bfloat16),
        compiler_params=pltpu.CompilerParams(vmem_limit_bytes=24 * MIB),
        name="finish",
    )(ends, *code_parts, pltpu.with_memory_space_constraint(base, pltpu.VMEM), up)


def gathered(part, axis, size):
    held = [part]
    for step in range(1, size):
        held.append(lax.ppermute(part, axis, [(i, (i + step) % size) for i in range(size)]))
    return held


def after(x, earlier):
    return lax.optimization_barrier((x, earlier))


def exchange(adapter_ids, owner_map, down_pool, up_pool):
    rows = adapter_ids.shape[0]
    width = down_pool.shape[2]
    most = width // 4 * 3
    names = {
        "4": (4, 0, width, 1), "7a": (7, 0, most, 1), "1": (1, 0, width, 1),
        "5": (5, 0, width, 1), "6a": (6, 0, most, 1), "2": (2, 0, width, 1),
        "3": (3, 0, width, 1), "6b": (6, most, width, 0), "7b": (7, most, width, 0),
    }
    sends = pick(list(names.values()), adapter_ids, owner_map, down_pool, up_pool)
    sends = dict(zip(names, sends))
    got = {}

    def swap(name, earlier=None):
        send = sends[name]
        if earlier is not None:
            send, got[earlier] = after(send, got[earlier])
        pairs = [(i, i ^ names[name][0]) for i in range(rows)]
        got[name] = lax.ppermute(send, "dp", pairs)

    for name, earlier in (
        ("4", None), ("7a", None), ("5", "7a"), ("1", "7a"), ("6a", "4"), ("2", "1"),
        ("3", "2"), ("6b", "6a"), ("7b", "5"),
    ):
        swap(name, earlier)
    return got, most


def shards(sizes, tokens, key_weight, down_pool, up_pool, adapter_ids, lengths, owner_map):
    n_groups, n_dp, n_tensor = sizes
    held, _, width = down_pool.shape
    columns = up_pool.shape[2]
    member = lax.axis_index("dp")
    by_swaps = n_dp == 8 and width % 512 == 0

    late_tokens = tokens
    if by_swaps:
        got, most = exchange(adapter_ids, owner_map, down_pool, up_pool)
        late_tokens, got["2"] = after(tokens, got["2"])

    me = lax.axis_index("tensor")
    base = None
    for step in reversed(range(n_tensor)):
        to = lax.rem(me + step, n_tensor)
        weight = lax.dynamic_slice_in_dim(key_weight, to * columns, columns, 1)
        part = jnp.dot(late_tokens, weight, preferred_element_type=jnp.float32)
        if step:
            part = lax.ppermute(
                part, "tensor", [(i, (i + step) % n_tensor) for i in range(n_tensor)]
            )
        base = part if base is None else base + part
    my_ids = lax.dynamic_index_in_dim(adapter_ids, member, 0, keepdims=False)
    my_slots = owner_map[my_ids]
    owners = my_slots // held
    ends = jnp.cumsum(lengths[0]).astype(jnp.int32)

    if by_swaps:
        index = jnp.concatenate([owners ^ member, my_slots % held])
        base, got["7a"], index = lax.optimization_barrier((base, got["7a"], index))

        def sources(first, up_first, six, seven):
            mine = [("pool", (down_pool, up_pool), first, 0)]
            near = [("plain", (got[str(s)],), first, width) for s in range(1, 6)]
            return mine + near + [("plain", (got[name],), *at) for name, *at in (six, seven)]

        most_of = sources(0, width, ("6a", 0, most), ("7a", 0, most))
        rest_of = sources(most, width, ("6b", 0, 0), ("7b", 0, 0))
        step = width // 4
        code, up = codes(index, ends, tokens, most_of, (0, most), step, columns)
        (code,) = codes(index, ends, tokens, rest_of, (most, width), step, before=code)
    else:
        blocks = dense(adapter_ids, owner_map, down_pool, up_pool)
        index = jnp.concatenate([owners, owners])
        whole = [("several", (blocks,), 0, width)]
        code, up = codes(index, ends, tokens, whole, (0, width), width, columns)
    code_parts = gathered(code, "tensor", n_tensor)
    return finish(ends, code_parts, base, up)


def solution(mesh):
    placed = (
        P(("groups", "dp"), "tensor"),
        P("tensor", None),
        P("dp", None, "tensor"),
        P("dp", None, "tensor"),
        P("groups", None),
        P(("groups", "dp"), None),
        P("groups"),
    )
    sizes = tuple(mesh.shape[name] for name in ("groups", "dp", "tensor"))
    return jax.shard_map(
        functools.partial(shards, sizes),
        mesh=mesh,
        in_specs=placed,
        out_specs=P(("groups", "dp"), "tensor"),
        check_vma=False,
    )
```

time: 138 us -> 184 us (1.33)
  waiting for transfers between devices: 81.4 us -> 128 us
  starting transfers between devices: 13.9 us -> 16.5 us
  Pallas kernels: 12.5 us -> 14.7 us
    ppermute x7 -> x9, waiting for transfers between devices: 80.2 us -> 127 us  [swap(): got[name] = lax.ppermute(send, 'dp', pairs)]
    squeeze x2 -> x0, local copies, waits for them, and re-layouts: 3.36 us -> none  [the longest x1 1.88 us: shards(): own_down = lax.dynamic_index_in_dim(down_pool, own, 0, keepdims=False)]
    pallas_call x2 -> x3, Pallas kernels: 10.2 us -> 12.3 us  [the longest x2 10.2 us: codes(): pl.pallas_call(functools.partial(code_kernel, count, cut, step, kinds, co...]
    unnamed x14 -> x22, local copies, waits for them, and re-layouts: 2.17 us -> 3.76 us
    ppermute x7 -> x9, starting transfers between devices: 11.7 us -> 12.4 us  [swap(): got[name] = lax.ppermute(send, 'dp', pairs)]
  transfers between devices with their start and end apart: 9 -> 11, of which waited for: 7 -> 8; matrix products, arithmetic and copies ran while one was open for 12% -> 6% of each run, Pallas kernels for 0% -> 3%
where the time goes in v5:
time: 184 us; the launch traced here: 185 us
  waiting for transfers between devices  128 us (70%)
  matrix products  20.2 us (11%)
  starting transfers between devices  16.5 us (9%)
  Pallas kernels  14.7 us (8%)
  local copies, waits for them, and re-layouts  4.58 us (2%)
    ppermute x9, waiting for transfers between devices, swap(): got[name] = lax.ppermute(send, 'dp', pairs)  127 us
    dot_general x2, matrix products, shards(): part = jnp.dot(late_tokens, weight, preferred_element_type=jnp.float32)  20.2 us
    ppermute x9, starting transfers between devices, swap(): got[name] = lax.ppermute(send, 'dp', pairs)  12.4 us
    pallas_call x2, Pallas kernels, codes(): pl.pallas_call(functools.partial(code_kernel, count, cut, step, kinds, co...  10.2 us
    unnamed x22, local copies, waits for them, and re-layouts  3.76 us
  transfers between devices with their start and end apart: 11, of which 8 were waited for; matrix products, arithmetic and copies ran while one was open for 6% of the time, Pallas kernels for 3%

profile of v5, /device:TPU:9, one launch (start us, length us, event | category | flops | bytes accessed | tf_op | source)
XLA Modules:
  0.0 184.5 jit_solution(8717009850177500106)
XLA Ops:
  0.0 0.7 copy-done
  0.7 0.7 copy-done.3
  1.3 2.1 %pick.1 = (bf16[64,4608]{1,0:T(8,128)(2,1)}, bf16[64,3584]{1,0:T(8,128)(2,1)S(1)}, bf16[64,4608]{1,0:T(8,128)(2,1)S(1)}, bf16[64,4608]{1,0:T(8,128)(2,1)S(1)}, b...) custom-call(s32[4,8]{1,0:T(4,128)S(1)} %bitcast.11, ...), custom_call_target="tpu_custom_call" | custom-call | tf_op jit(solution)/shard_map/pick/pallas_call | solution.py:63
  3.5 0.8 copy-done.5
  4.3 0.8 copy-done.6
  5.1 0.8 copy-done.7
  5.9 2.8 %collective-permute-start = (bf16[64,3584]{1,0:T(8,128)(2,1)S(1)}, bf16[64,3584]{1,0:T(8,128)(2,1)S(1)}, u32[]{:S(2)}, u32[]{:S(2)}) collective-permute-start(bf16[64,3584]{1,0:T(8,128)(2,1)S(1)} %get-tuple-element.39), channel_id=1, source_target_pairs={{0,14},{2,12},{4,10},{6,8},{8,6},{10,4},{12,2},{14,0},{1,15},{3,13... | collective-permute-start | bytes 1376264 | tf_op jit(solution)/shard_map/ppermute | solution.py:314
  8.6 20.1 %collective-permute-done.refs_8_ = bf16[64,3584]{1,0:T(8,128)(2,1)S(1)} collective-permute-done((bf16[64,3584]{1,0:T(8,128)(2,1)S(1)}, bf16[64,3584]{1,0:T(8,128)(2,1)S(1)}, u32[]{:S(2)}, u32[]{:S(2)}) %collective-permute-start) | collective-permute-done | bytes 458784 | tf_op jit(solution)/shard_map/ppermute | solution.py:314
  28.7 2.9 %collective-permute-start.1 = (bf16[64,4608]{1,0:T(8,128)(2,1)S(1)}, bf16[64,4608]{1,0:T(8,128)(2,1)S(1)}, u32[]{:S(2)}, u32[]{:S(2)}) collective-permute-start(bf16[64,4608]{1,0:T(8,128)(2,1)S(1)} %get-tuple-element.41), channel_id=1, source_target_pairs={{0,2},{2,0},{4,6},{6,4},{8,10},{10,8},{12,14},{14,12},{1,3},{3,1},... | collective-permute-start | bytes 1769480 | tf_op jit(solution)/shard_map/ppermute | solution.py:314
  31.7 13.3 %collective-permute-done.1.refs_2_ = bf16[64,4608]{1,0:T(8,128)(2,1)S(1)} collective-permute-done((bf16[64,4608]{1,0:T(8,128)(2,1)S(1)}, bf16[64,4608]{1,0:T(8,128)(2,1)S(1)}, u32[]{:S(2)}, u32[]{:S(2)}) %collective-permute-start.1) | collective-permute-done | bytes 589856 | tf_op jit(solution)/shard_map/ppermute | solution.py:314
  44.9 13.8 %collective-permute-done.2.refs_3_ = bf16[64,4608]{1,0:T(8,128)(2,1)S(1)} collective-permute-done((bf16[64,4608]{1,0:T(8,128)(2,1)S(1)}, bf16[64,4608]{1,0:T(8,128)(2,1)S(1)}, u32[]{:S(2)}, u32[]{:S(2)}) %collective-permute-start.2) | collective-permute-done | bytes 589856 | tf_op jit(solution)/shard_map/ppermute | solution.py:314
  58.7 10.4 %fusion.2 = f32[1024,512]{1,0:T(8,128)} fusion(bf16[1024,4096]{1,0:T(8,128)(2,1)} %tokens.3, bf16[4096,1024]{1,0:T(8,128)(2,1)} %param.8, s32[]{:T(128)S(6)} %select_n.32), kind=kOutput, calls=%fused_computation.3 | convolution fusion | flops 4294967296 | bytes 14680068 | tf_op jit(solution)/shard_map/dot_general | solution.py:341
  69.2 1.9 %collective-permute-start.3 = (f32[1024,512]{1,0:T(8,128)}, f32[1024,512]{1,0:T(8,128)}, u32[]{:S(2)}, u32[]{:S(2)}) collective-permute-start(f32[1024,512]{1,0:T(8,128)} %fusion.2), channel_id=1, source_target_pairs={{0,1},{1,0},{2,3},{3,2},{4,5},{5,4},{6,7},{7,6},{8,9},{9,8},{10,11... | collective-permute-start | bytes 6291464 | tf_op jit(solution)/shard_map/ppermute | solution.py:343
  71.1 0.2 dynamic-slice_reduce_fusion
  71.3 3.3 %collective-permute-start.6 = (bf16[64,4608]{1,0:T(8,128)(2,1)}, bf16[64,4608]{1,0:T(8,128)(2,1)S(1)}, u32[]{:S(2)}, u32[]{:S(2)}) collective-permute-start(bf16[64,4608]{1,0:T(8,128)(2,1)} %copy-done.6), channel_id=1, source_target_pairs={{0,10},{2,8},{4,14},{6,12},{8,2},{10,0},{12,6},{14,4},{1,11},{3,9}... | collective-permute-start | bytes 1769480 | tf_op jit(solution)/shard_map/ppermute | solution.py:314
  74.6 35.0 %collective-permute-done.5.refs_5_ = bf16[64,4608]{1,0:T(8,128)(2,1)S(1)} collective-permute-done((bf16[64,4608]{1,0:T(8,128)(2,1)}, bf16[64,4608]{1,0:T(8,128)(2,1)S(1)}, u32[]{:S(2)}, u32[]{:S(2)}) %collective-permute-start.5) | collective-permute-done | bytes 589856 | tf_op jit(solution)/shard_map/ppermute | solution.py:314
  109.5 1.1 collective-permute-start.7
  110.7 0.6 gather_fusion
  111.3 0.2 reduce-window.9
  111.5 0.1 pad_add_fusion.index
  111.6 20.4 %collective-permute-done.6.refs_6_ = bf16[64,4608]{1,0:T(8,128)(2,1)S(1)} collective-permute-done((bf16[64,4608]{1,0:T(8,128)(2,1)}, bf16[64,4608]{1,0:T(8,128)(2,1)S(1)}, u32[]{:S(2)}, u32[]{:S(2)}) %collective-permute-start.6) | collective-permute-done | bytes 589856 | tf_op jit(solution)/shard_map/ppermute | solution.py:314
  132.0 17.2 %collective-permute-done.7.refs_7_ = bf16[64,3584]{1,0:T(8,128)(2,1)S(1)} collective-permute-done((bf16[64,3584]{1,0:T(8,128)(2,1)}, bf16[64,3584]{1,0:T(8,128)(2,1)S(1)}, u32[]{:S(2)}, u32[]{:S(2)}) %collective-permute-start.7) | collective-permute-done | bytes 458784 | tf_op jit(solution)/shard_map/ppermute | solution.py:314
  149.2 0.4 collective-permute-start.8
  149.6 2.0 %collective-permute-start.9 = (bf16[64,1024]{1,0:T(8,128)(2,1)S(1)}, bf16[64,1024]{1,0:T(8,128)(2,1)S(1)}, u32[]{:S(2)}, u32[]{:S(2)}) collective-permute-start(bf16[64,1024]{1,0:T(8,128)(2,1)S(1)} %get-tuple-element.59), channel_id=1, source_target_pairs={{0,14},{2,12},{4,10},{6,8},{8,6},{10,4},{12,2},{14,0},{1,15},{3,13... | collective-permute-start | bytes 393224 | tf_op jit(solution)/shard_map/ppermute | solution.py:314
  151.5 0.0 collective-permute-start.4
  151.5 9.8 %fusion.4.refs_2_ = f32[1024,512]{1,0:T(8,128)S(1)} fusion(f32[1024,512]{1,0:T(8,128)} %collective-permute-done.3, bf16[1024,4096]{1,0:T(8,128)(2,1)} %tokens.3, bf16[4096,1024]{1,0:T(8,128)(2,1)} %param.8, s32[]{:T(128)S(6)} %select_n.33), kind=kOutput, calls=%fused_computation.5 | convolution fusion | flops 4295491584 | bytes 16777220 | tf_op jit(solution)/shard_map/dot_general | solution.py:341
  161.3 7.3 %collective-permute-done.4.refs_4_ = bf16[64,4608]{1,0:T(8,128)(2,1)S(1)} collective-permute-done((bf16[64,4608]{1,0:T(8,128)(2,1)}, bf16[64,4608]{1,0:T(8,128)(2,1)S(1)}, u32[]{:S(2)}, u32[]{:S(2)}) %collective-permute-start.4) | collective-permute-done | bytes 589856 | tf_op jit(solution)/shard_map/ppermute | solution.py:314
  168.6 6.4 %codes.2 = (f32[512,128]{1,0:T(8,128)S(1)}, bf16[256,512]{1,0:T(8,128)(2,1)S(1)}) custom-call(s32[8]{0:T(128)S(1)} %pad_add_fusion.index, s32[4]{0:T(128)S(1)} %bitcast.12, bf16[1024,4096]{1,0:T(8,128)(2,1)} %tokens.3, bf16[10,64,4096]{2,1,0:T(8,128)(2,1)S(1)} %bitcast.10, bf16[10,64,512]{2,1,0:T(8,128)(2,1)S(1)} %copy-done.2, ...), custom_call_target="tpu_custom_call" | custom-call | flops 1610612736 | bytes 7864320 | tf_op jit(solution)/shard_map/codes/pallas_call | solution.py:205
  175.1 3.7 %codes.3.refs_0_ = f32[512,128]{1,0:T(8,128)S(1)} custom-call(s32[8]{0:T(128)S(1)} %pad_add_fusion.index, s32[4]{0:T(128)S(1)} %bitcast.13, bf16[1024,4096]{1,0:T(8,128)(2,1)} %tokens.3, bf16[10,64,4096]{2,1,0:T(8,128)(2,1)S(1)} %bitcast.10, bf16[10,64,512]{2,1,0:T(8,128)(2,1)S(1)} %copy-done.2, bf16[64,4608]{1,0:T(8,128)(2,1)S(1)} %collective-permute-done.1.refs_2_, ...), custom_call_target="tpu_custom_call" | custom-call | flops 536870912 | bytes 2621440 | tf_op jit(solution)/shard_map/codes/pallas_call | solution.py:205
  178.8 2.1 %collective-permute-start.10 = (f32[512,128]{1,0:T(8,128)S(1)}, f32[512,128]{1,0:T(8,128)S(1)}, u32[]{:S(2)}, u32[]{:S(2)}) collective-permute-start(f32[512,128]{1,0:T(8,128)S(1)} %codes.3.refs_0_), channel_id=1, source_target_pairs={{0,1},{1,0},{2,3},{3,2},{4,5},{5,4},{6,7},{7,6},{8,9},{9,8},{10,11... | collective-permute-start | bytes 786440 | tf_op jit(solution)/shard_map/ppermute | solution.py:288
  181.0 1.2 collective-permute-done.10.refs_1_
  182.1 2.4 %finish.1 = bf16[1024,512]{1,0:T(8,128)(2,1)} custom-call(s32[4]{0:T(128)S(1)} %bitcast.14, f32[512,128]{1,0:T(8,128)S(1)} %codes.3.refs_0_, f32[512,128]{1,0:T(8,128)S(1)} %collective-permute-done.10.refs_1_, f32[1024,512]{1,0:T(8,128)S(1)} %fusion.4.refs_2_, bf16[256,512]{1,0:T(8,128)(2,1)S(1)} %get-tuple-element.64.refs_3_), custom_call_target="tpu_custom_call" | custom-call | tf_op jit(solution)/shard_map/finish/pallas_call | solution.py:267
  (26 shorter events, 0.1 us)
Async XLA Ops:
  0.0 0.7 copy-start
  0.7 0.7 copy-start.3
  3.4 0.8 copy-start.5
  4.3 0.8 copy-start.6
  5.1 0.8 copy-start.7
  5.9 22.9 %collective-permute-start = (bf16[64,3584]{1,0:T(8,128)(2,1)S(1)}, bf16[64,3584]{1,0:T(8,128)(2,1)S(1)}, u32[]{:S(2)}, u32[]{:S(2)}) collective-permute-start(bf16[64,3584]{1,0:T(8,128)(2,1)S(1)} %get-tuple-element.39), channel_id=1, source_target_pairs={{0,14},{2,12},{4,10},{6,8},{8,6},{10,4},{12,2},{14,0},{1,15},{3,13... | collective-permute-start | bytes 1376264 | tf_op jit(solution)/shard_map/ppermute | solution.py:314
  28.7 16.2 %collective-permute-start.1 = (bf16[64,4608]{1,0:T(8,128)(2,1)S(1)}, bf16[64,4608]{1,0:T(8,128)(2,1)S(1)}, u32[]{:S(2)}, u32[]{:S(2)}) collective-permute-start(bf16[64,4608]{1,0:T(8,128)(2,1)S(1)} %get-tuple-element.41), channel_id=1, source_target_pairs={{0,2},{2,0},{4,6},{6,4},{8,10},{10,8},{12,14},{14,12},{1,3},{3,1},... | collective-permute-start | bytes 1769480 | tf_op jit(solution)/shard_map/ppermute | solution.py:314
  44.9 13.8 %collective-permute-start.2 = (bf16[64,4608]{1,0:T(8,128)(2,1)S(1)}, bf16[64,4608]{1,0:T(8,128)(2,1)S(1)}, u32[]{:S(2)}, u32[]{:S(2)}) collective-permute-start(bf16[64,4608]{1,0:T(8,128)(2,1)S(1)} %get-tuple-element.42), channel_id=1, source_target_pairs={{0,4},{2,6},{4,0},{6,2},{8,12},{10,14},{12,8},{14,10},{1,5},{3,7},... | collective-permute-start | bytes 1769480 | tf_op jit(solution)/shard_map/ppermute | solution.py:314
  58.7 12.4 %copy-start.4 = (s32[8,4]{0,1:T(4,128)S(1)}, s32[8,4]{0,1:T(4,128)}, u32[]{:S(2)}) copy-start(s32[8,4]{0,1:T(4,128)} %param.11) | copy-start | bytes 388
  58.7 51.9 %copy-start.1 = (s32[80]{0:T(128)S(1)}, s32[80]{0:T(128)}, u32[]{:S(2)}) copy-start(s32[80]{0:T(128)} %owner_map.1) | copy-start | bytes 964
  58.7 52.6 %copy-start.8 = (s32[1,4]{1,0:T(1,128)S(1)}, s32[1,4]{1,0:T(1,128)}, u32[]{:S(2)}) copy-start(s32[1,4]{1,0:T(1,128)} %param.12) | copy-start | bytes 52
  69.2 82.4 %collective-permute-start.3 = (f32[1024,512]{1,0:T(8,128)}, f32[1024,512]{1,0:T(8,128)}, u32[]{:S(2)}, u32[]{:S(2)}) collective-permute-start(f32[1024,512]{1,0:T(8,128)} %fusion.2), channel_id=1, source_target_pairs={{0,1},{1,0},{2,3},{3,2},{4,5},{5,4},{6,7},{7,6},{8,9},{9,8},{10,11... | collective-permute-start | bytes 6291464 | tf_op jit(solution)/shard_map/ppermute | solution.py:343
  71.1 38.4 %collective-permute-start.5 = (bf16[64,4608]{1,0:T(8,128)(2,1)}, bf16[64,4608]{1,0:T(8,128)(2,1)S(1)}, u32[]{:S(2)}, u32[]{:S(2)}) collective-permute-start(bf16[64,4608]{1,0:T(8,128)(2,1)} %get-tuple-element.51), channel_id=1, source_target_pairs={{0,8},{2,10},{4,12},{6,14},{8,0},{10,2},{12,4},{14,6},{1,9},{3,11}... | collective-permute-start | bytes 1769480 | tf_op jit(solution)/shard_map/ppermute | solution.py:314
  71.3 60.7 %collective-permute-start.6 = (bf16[64,4608]{1,0:T(8,128)(2,1)}, bf16[64,4608]{1,0:T(8,128)(2,1)S(1)}, u32[]{:S(2)}, u32[]{:S(2)}) collective-permute-start(bf16[64,4608]{1,0:T(8,128)(2,1)} %copy-done.6), channel_id=1, source_target_pairs={{0,10},{2,8},{4,14},{6,12},{8,2},{10,0},{12,6},{14,4},{1,11},{3,9}... | collective-permute-start | bytes 1769480 | tf_op jit(solution)/shard_map/ppermute | solution.py:314
  109.5 39.6 %collective-permute-start.7 = (bf16[64,3584]{1,0:T(8,128)(2,1)}, bf16[64,3584]{1,0:T(8,128)(2,1)S(1)}, u32[]{:S(2)}, u32[]{:S(2)}) collective-permute-start(bf16[64,3584]{1,0:T(8,128)(2,1)} %copy-done.7), channel_id=1, source_target_pairs={{0,12},{2,14},{4,8},{6,10},{8,4},{10,6},{12,0},{14,2},{1,13},{3,15... | collective-permute-start | bytes 1376264 | tf_op jit(solution)/shard_map/ppermute | solution.py:314
  149.2 19.4 %slice-start = ((s8[5242880]{0:T(1024)(128)(4,1)}), s8[4194304]{0:T(1024)(128)(4,1)S(1)}, s32[]{:S(2)}) async-start(s8[5242880]{0:T(1024)(128)(4,1)} %bitcast.9), calls=%async_computation | async-start | bytes 8388608
  149.2 19.4 %slice-start.1 = ((s8[5242880]{0:T(1024)(128)(4,1)}), s8[1048576]{0:T(1024)(128)(4,1)S(1)}, s32[]{:S(2)}) async-start(s8[5242880]{0:T(1024)(128)(4,1)} %bitcast.9), calls=%async_computation.1 | async-start | bytes 2097152
  149.2 19.4 %copy-start.2 = (bf16[10,64,512]{2,1,0:T(8,128)(2,1)S(1)}, bf16[10,64,512]{2,1,0:T(8,128)(2,1)}, u32[]{:S(2)}) copy-start(bf16[10,64,512]{2,1,0:T(8,128)(2,1)} %refs_1_.3) | copy-start | bytes 1966084
  149.2 25.9 %collective-permute-start.8 = (bf16[64,1024]{1,0:T(8,128)(2,1)S(1)}, bf16[64,1024]{1,0:T(8,128)(2,1)S(1)}, u32[]{:S(2)}, u32[]{:S(2)}) collective-permute-start(bf16[64,1024]{1,0:T(8,128)(2,1)S(1)} %get-tuple-element.58), channel_id=1, source_target_pairs={{0,12},{2,14},{4,8},{6,10},{8,4},{10,6},{12,0},{14,2},{1,13},{3,15... | collective-permute-start | bytes 393224 | tf_op jit(solution)/shard_map/ppermute | solution.py:314
  149.6 25.5 %collective-permute-start.9 = (bf16[64,1024]{1,0:T(8,128)(2,1)S(1)}, bf16[64,1024]{1,0:T(8,128)(2,1)S(1)}, u32[]{:S(2)}, u32[]{:S(2)}) collective-permute-start(bf16[64,1024]{1,0:T(8,128)(2,1)S(1)} %get-tuple-element.59), channel_id=1, source_target_pairs={{0,14},{2,12},{4,10},{6,8},{8,6},{10,4},{12,2},{14,0},{1,15},{3,13... | collective-permute-start | bytes 393224 | tf_op jit(solution)/shard_map/ppermute | solution.py:314
  151.5 17.1 %collective-permute-start.4 = (bf16[64,4608]{1,0:T(8,128)(2,1)}, bf16[64,4608]{1,0:T(8,128)(2,1)S(1)}, u32[]{:S(2)}, u32[]{:S(2)}) collective-permute-start(bf16[64,4608]{1,0:T(8,128)(2,1)} %copy-done.5), channel_id=1, source_target_pairs={{0,6},{2,4},{4,2},{6,0},{8,14},{10,12},{12,10},{14,8},{1,7},{3,5},... | collective-permute-start | bytes 1769480 | tf_op jit(solution)/shard_map/ppermute | solution.py:314
  178.8 3.3 %collective-permute-start.10 = (f32[512,128]{1,0:T(8,128)S(1)}, f32[512,128]{1,0:T(8,128)S(1)}, u32[]{:S(2)}, u32[]{:S(2)}) collective-permute-start(f32[512,128]{1,0:T(8,128)S(1)} %codes.3.refs_0_), channel_id=1, source_target_pairs={{0,1},{1,0},{2,3},{3,2},{4,5},{5,4},{6,7},{7,6},{8,9},{9,8},{10,11... | collective-permute-start | bytes 786440 | tf_op jit(solution)/shard_map/ppermute | solution.py:288
